TPU v7x, 512 devices: a whole 4x4x16 slice. The times are simulated.
512 devices in a mesh: tile: 128 (over z, x, core), depth: 4 (over y).
Axes of the slice: x: 4, y: 4, z: 16, core: 2. Of those that a mesh axis runs over, the one named last changes fastest.
Arguments:
- substrate_start: float32 [4, 2, 16, 256, 1024], P(None, None, 'depth', 'tile'), may hold values from -6 to 6
- adatom_start: float32 [40, 2, 393216], P(None, None, ('tile', 'depth')), may hold values from -6 to 6
- disorder: float32 [16, 256, 1024], P('depth', 'tile'), may hold values from -0.4 to 0.4
- adatom_block: float32 [40, 40], replicated, as said below
- coupling: float32 [4, 40], replicated, may hold values from -1 to 1
- adatom_tile: int32 [393216, 1], P(('tile', 'depth')), may hold values from 0 to 127; in each aligned block of 768 rows (0 to 767, 768 to 1535, ...) at most 12 rows name the same one
- adatom_spot: int32 [393216], P(('tile', 'depth')), may hold values from 0 to 2047
Outputs:
- substrate_prev: float32 [4, 2, 16, 256, 1024], P(None, None, 'depth', 'tile')
- substrate_last: float32 [4, 2, 16, 256, 1024], P(None, None, 'depth', 'tile')
- adatom_prev: float32 [40, 2, 393216], P(None, None, ('tile', 'depth'))
- adatom_last: float32 [40, 2, 393216], P(None, None, ('tile', 'depth'))
Inputs may be any that keep to these rules, and one draw needn't show every extreme that they name: `adatom_tile`: among the adatoms of one device, no tile is named by more than 12. adatom_block is symmetric.
All inputs are finite; a program needn't handle non-finite values.
Results may differ from a plain program's by a relative error of at most 0.0003.
Values sent between devices are 32-bit elements; how exact they have to be, the bound alone decides.
No kernel may reach another device: no remote copies, remote signals or barrier semaphores. Data moves between devices by JAX's collectives and lax.ppermute only.
A program may use at most 64 MiB of HBM per device.

v0:
```python
import jax
import jax.numpy as jnp
from jax import lax
from jax.sharding import PartitionSpec as P

STEPS = 3


hopping = 0.12
chemical = 0.15
pairing = 0.3


def extended(shard, sides, width):
    for axis, dim in sides:
        size, length = (lax.axis_size(axis), shard.shape[dim])
        up = [(i, (i + 1) % size) for i in range(size - 1)]
        down = [(j, i) for i, j in up]
        last = lax.slice_in_dim(shard, length - width, length, axis=dim)
        first = lax.slice_in_dim(shard, 0, width, axis=dim)
        before = lax.ppermute(last, axis, up)
        after = lax.ppermute(first, axis, down)
        shard = jnp.concatenate([before, shard, after], axis=dim)
    return shard


def broadcast(shard, axis, root):
    mine = lax.axis_index(axis) == root
    return lax.psum(jnp.where(mine, shard, jnp.zeros_like(shard)), axis)


def substrate_terms(padded, field, disorder):
    beside = padded[:, :, 2:, 1:-1] + padded[:, :, :-2, 1:-1]
    beside = beside + padded[:, :, 1:-1, 2:] + padded[:, :, 1:-1, :-2]
    widened = jnp.pad(field, ((0, 0), (0, 0), (0, 0), (0, 0), (1, 1)))
    beside = beside + widened[..., 2:] + widened[..., :-2]
    signs = jnp.array([1.0, 1.0, -1.0, -1.0], jnp.float32).reshape(4, 1, 1, 1, 1)
    onsite = (disorder - chemical)[None, None] * field - hopping * beside
    partner = jnp.concatenate([field[2:], field[:2]], axis=0)
    return signs * onsite + pairing * partner


def per_device(
    substrate_start, adatom_start, disorder, adatom_block, coupling, adatom_tile, adatom_spot
):
    tiles = lax.axis_size("tile")
    count = adatom_spot.shape[0]
    capacity = 2 * count // tiles
    orbs, vecs, local_layers, rows, cols = substrate_start.shape
    width = orbs * vecs
    spots_n = rows * cols
    slots_n = tiles * capacity
    own_tile = adatom_tile[:, 0]
    onehot = (own_tile[:, None] == jnp.arange(tiles, dtype=jnp.int32)[None, :]).astype(jnp.bfloat16)
    lower = (
        lax.broadcasted_iota(jnp.int32, (count, count), 0)
        > lax.broadcasted_iota(jnp.int32, (count, count), 1)
    ).astype(jnp.bfloat16)
    before = jnp.dot(lower, onehot, preferred_element_type=jnp.float32)
    rank = jnp.sum(before * onehot.astype(jnp.float32), axis=1).astype(jnp.int32)
    slot = own_tile * capacity + rank
    sent_spots = (
        jnp.zeros((slots_n,), jnp.int32).at[slot].set(adatom_spot + 1).reshape(tiles, capacity)
    )
    got_spots = lax.all_to_all(sent_spots, "tile", split_axis=0, concat_axis=0, tiled=True).reshape(
        -1
    )
    row_index = jnp.maximum(got_spots - 1, 0)
    live = (got_spots > 0).astype(jnp.float32)
    on_top = lax.axis_index("depth") == 0

    def apply(sub, adatoms):
        padded = extended(sub, (("tile", 3), ("depth", 2)), 1)
        sub_out = substrate_terms(padded, sub, disorder)
        surface = sub[:, :, 0].reshape(width, spots_n)
        contrib = jnp.einsum(
            "oa,avn->nov", coupling, adatoms, precision=lax.Precision.HIGHEST
        ).reshape(count, width)
        sent = (
            jnp.zeros((slots_n, width), jnp.float32)
            .at[slot]
            .set(contrib)
            .reshape(tiles, capacity, width)
        )
        got = lax.all_to_all(sent, "tile", split_axis=0, concat_axis=0, tiled=True).reshape(
            slots_n, width
        )
        shared = broadcast(surface, "depth", 0)
        answer = jnp.take(shared, row_index, axis=1).T * live[:, None]
        local_add = jnp.zeros((spots_n, width), jnp.float32).at[row_index].add(got)
        added = lax.psum(local_add, "depth")
        back = lax.all_to_all(
            answer.reshape(tiles, capacity, width), "tile", split_axis=0, concat_axis=0, tiled=True
        ).reshape(slots_n, width)
        below = back[slot].T.reshape(orbs, vecs, count)
        ad_out = jnp.einsum("ab,bvn->avn", adatom_block, adatoms, precision=lax.Precision.HIGHEST)
        ad_out = ad_out + jnp.einsum(
            "oa,ovn->avn", coupling, below, precision=lax.Precision.HIGHEST
        )
        top_add = jnp.where(on_top, added, 0.0).T.reshape(orbs, vecs, rows, cols)
        sub_out = sub_out.at[:, :, 0].add(top_add)
        return (sub_out, ad_out)

    prev_sub, prev_ad = (substrate_start, adatom_start)
    cur_sub, cur_ad = apply(prev_sub, prev_ad)
    for step in range(STEPS - 1):
        new_sub, new_ad = apply(cur_sub, cur_ad)
        new_sub = 2.0 * new_sub - prev_sub
        new_ad = 2.0 * new_ad - prev_ad
        prev_sub, prev_ad = (cur_sub, cur_ad)
        cur_sub, cur_ad = (new_sub, new_ad)
    return (prev_sub, cur_sub, prev_ad, cur_ad)


def solution(mesh):
    in_specs = (
        P(None, None, "depth", "tile", None),
        P(None, None, ("tile", "depth")),
        P("depth", "tile", None),
        P(),
        P(),
        P(("tile", "depth"), None),
        P(("tile", "depth")),
    )
    out_specs = (
        P(None, None, "depth", "tile", None),
        P(None, None, "depth", "tile", None),
        P(None, None, ("tile", "depth")),
        P(None, None, ("tile", "depth")),
    )
    return jax.shard_map(
        per_device, mesh=mesh, in_specs=in_specs, out_specs=out_specs, check_vma=False
    )
```

profile of v0, /device:TPU:7, one launch (start us, length us, event | category | flops | bytes accessed | tf_op | source)
XLA Modules:
  0.0 618.7 jit_solution(14415956502742465969)
XLA Ops:
  7.2 0.7 reduce.6
  8.5 3.4 scatter_custom_fusion
  12.6 19.7 %all-to-all-start = ((s32[128,1,12]{2,1,0:T(1,128)}), s32[128,1,12]{2,1,0:T(1,128)S(1)}, u32[]{:S(2)}, u32[]{:S(2)}) async-start(s32[128,1,12]{2,1,0:T(1,128)} %bitcast), calls=%async_computation | async-start | bytes 131072 | tf_op jit(solution)/shard_map/all_to_all | solution.py:65
  32.5 3.3 collective-permute-start
  35.9 1.9 collective-permute-start.1
  38.4 4.4 scatter_custom_fusion.1
  43.6 1.1 copy.122
  44.7 1.3 copy.128
  46.1 17.3 %all-to-all-start.1 = ((f32[128,12,8]{1,2,0:T(8,128)}), f32[128,12,8]{1,2,0:T(8,128)S(1)}, u32[]{:S(2)}, u32[]{:S(2)}) async-start(f32[128,12,8]{1,2,0:T(8,128)} %copy.122), calls=%async_computation.1 | async-start | bytes 1048576 | tf_op jit(solution)/shard_map/all_to_all | solution.py:85
  64.0 1.3 collective-permute-start.2
  65.3 4.2 collective-permute-start.3
  69.8 26.5 %all-to-all-done.1 = f32[128,12,8]{1,2,0:T(8,128)S(1)} async-done(((f32[128,12,8]{1,2,0:T(8,128)}), f32[128,12,8]{1,2,0:T(8,128)S(1)}, u32[]{:S(2)}, u32[]{:S(2)}) %all-to-all-start.1) | async-done | bytes 49184 | tf_op jit(solution)/shard_map/all_to_all | solution.py:85
  96.9 9.8 %scatter_custom_fusion.2 = f32[2048,8]{1,0:T(8,128)} fusion(s32[1536]{0:T(1024)S(1)} %reshape.342, f32[1536,8]{1,0:T(8,128)S(1)} %copy.124, f32[]{:T(128)} %constant.103.clone.1), kind=kCustom, calls=%fused_computation.43 | custom fusion | flops 12288 | bytes 65540 | tf_op jit(solution)/shard_map/scatter-add | solution.py:90
  107.4 1.2 fusion.40
  108.5 64.5 %all-reduce.14.cloned.1.call-done = (f32[2048,8]{1,0:T(8,128)}, f32[8,2048]{0,1:T(8,128)}) async-done(((f32[2048,8]{1,0:T(8,128)}, f32[8,2048]{0,1:T(8,128)}), (f32[2048,8]{1,0:T(8,128)}, f32[8,2048]{0,1:T(8,128)})) %all-reduce.14.cloned.1.call-update) | async-done | bytes 131088 | tf_op jit(solution)/shard_map/psum | solution.py:91
  173.0 1.3 select_bitcast_fusion.2
  175.0 3.7 collective-permute-start.4
  178.7 1.9 collective-permute-start.5
  180.6 3.8 gather_fusion.3
  184.4 1.1 fusion.11
  186.3 1.1 copy.130
  187.5 17.6 %all-to-all-start.2 = ((f32[128,12,8]{1,2,0:T(8,128)}), f32[128,12,8]{1,2,0:T(8,128)S(1)}, u32[]{:S(2)}, u32[]{:S(2)}) async-start(f32[128,12,8]{1,2,0:T(8,128)} %copy.130), calls=%async_computation.2 | async-start | bytes 1048576 | tf_op jit(solution)/shard_map/all_to_all | solution.py:92
  205.1 1.3 copy.143
  206.7 1.3 collective-permute-start.6
  208.0 4.2 collective-permute-start.7
  212.2 25.8 %all-to-all-done.2 = f32[128,12,8]{1,2,0:T(8,128)S(1)} async-done(((f32[128,12,8]{1,2,0:T(8,128)}), f32[128,12,8]{1,2,0:T(8,128)S(1)}, u32[]{:S(2)}, u32[]{:S(2)}) %all-to-all-start.2) | async-done | bytes 49184 | tf_op jit(solution)/shard_map/all_to_all | solution.py:92
  238.7 1.6 gather_fusion
  241.6 4.4 scatter_custom_fusion.3
  246.8 1.1 copy.138
  247.9 7.0 %all-to-all-start.3 = ((f32[128,12,8]{1,2,0:T(8,128)}), f32[128,12,8]{1,2,0:T(8,128)S(1)}, u32[]{:S(2)}, u32[]{:S(2)}) async-start(f32[128,12,8]{1,2,0:T(8,128)} %copy.138), calls=%async_computation.3 | async-start | bytes 1048576 | tf_op jit(solution)/shard_map/all_to_all | solution.py:85
  255.0 32.8 %all-to-all-done.3 = f32[128,12,8]{1,2,0:T(8,128)S(1)} async-done(((f32[128,12,8]{1,2,0:T(8,128)}), f32[128,12,8]{1,2,0:T(8,128)S(1)}, u32[]{:S(2)}, u32[]{:S(2)}) %all-to-all-start.3) | async-done | bytes 49184 | tf_op jit(solution)/shard_map/all_to_all | solution.py:85
  288.5 10.1 %scatter_custom_fusion.4 = f32[2048,8]{1,0:T(8,128)} fusion(s32[1536]{0:T(1024)S(1)} %reshape.342, f32[1536,8]{1,0:T(8,128)S(1)} %copy.140, f32[]{:T(128)} %constant.103.clone.1), kind=kCustom, calls=%fused_computation.41 | custom fusion | flops 12288 | bytes 65540 | tf_op jit(solution)/shard_map/scatter-add | solution.py:90
  298.7 1.2 fusion.41
  299.9 62.4 %all-reduce.12.cloned.1.call-done = (f32[2048,8]{1,0:T(8,128)}, f32[8,2048]{0,1:T(8,128)}) async-done(((f32[2048,8]{1,0:T(8,128)}, f32[8,2048]{0,1:T(8,128)}), (f32[2048,8]{1,0:T(8,128)}, f32[8,2048]{0,1:T(8,128)})) %all-reduce.12.cloned.1.call-update) | async-done | bytes 131088 | tf_op jit(solution)/shard_map/psum | solution.py:91
  362.3 1.3 select_bitcast_fusion.1
  364.2 3.8 gather_fusion.4
  368.1 1.1 fusion.10
  370.0 1.1 copy.145
  371.1 16.8 %all-to-all-start.4 = ((f32[128,12,8]{1,2,0:T(8,128)}), f32[128,12,8]{1,2,0:T(8,128)S(1)}, u32[]{:S(2)}, u32[]{:S(2)}) async-start(f32[128,12,8]{1,2,0:T(8,128)} %copy.145), calls=%async_computation.4 | async-start | bytes 1048576 | tf_op jit(solution)/shard_map/all_to_all | solution.py:92
  388.1 3.3 collective-permute-start.8
  391.5 1.9 collective-permute-start.9
  394.2 1.3 copy.158
  395.5 12.7 %collective-permute-done.8 = f32[4,2,4,1,1024]{4,3,1,0,2:T(1,128)S(1)} collective-permute-done((f32[4,2,4,1,1024]{4,3,1,0,2:T(1,128)S(1)}, f32[4,2,4,1,1024]{4,3,1,0,2:T(1,128)S(1)}, u32[]{:S(2)}, u32[]{:S(2)}) %collective-permute-start.8) | collective-permute-done | bytes 131104 | tf_op jit(solution)/shard_map/ppermute | solution.py:21
  408.2 4.9 collective-permute-done.9
  413.2 1.3 collective-permute-start.10
  414.5 4.0 collective-permute-start.11
  418.5 2.3 all-to-all-done.4
  421.5 1.6 gather_fusion.1
  424.4 4.5 scatter_custom_fusion.5
  429.7 1.1 copy.154
  430.9 13.6 %all-to-all-start.5 = ((f32[128,12,8]{1,2,0:T(8,128)}), f32[128,12,8]{1,2,0:T(8,128)S(1)}, u32[]{:S(2)}, u32[]{:S(2)}) async-start(f32[128,12,8]{1,2,0:T(8,128)} %copy.154), calls=%async_computation.5 | async-start | bytes 1048576 | tf_op jit(solution)/shard_map/all_to_all | solution.py:85
  444.6 0.8 copy.167
  445.4 32.0 %all-to-all-done.5 = f32[128,12,8]{1,2,0:T(8,128)S(1)} async-done(((f32[128,12,8]{1,2,0:T(8,128)}), f32[128,12,8]{1,2,0:T(8,128)S(1)}, u32[]{:S(2)}, u32[]{:S(2)}) %all-to-all-start.5) | async-done | bytes 49184 | tf_op jit(solution)/shard_map/all_to_all | solution.py:85
  478.1 9.8 %scatter_custom_fusion.6 = f32[2048,8]{1,0:T(8,128)} fusion(s32[1536]{0:T(1024)S(1)} %reshape.342, f32[1536,8]{1,0:T(8,128)S(1)} %copy.156, f32[]{:T(128)} %constant.103.clone.1), kind=kCustom, calls=%fused_computation.39 | custom fusion | flops 12288 | bytes 65540 | tf_op jit(solution)/shard_map/scatter-add | solution.py:90
  487.9 1.2 fusion.42
  489.1 62.4 %all-reduce.10.cloned.1.call-done = (f32[2048,8]{1,0:T(8,128)}, f32[8,2048]{0,1:T(8,128)}) async-done(((f32[2048,8]{1,0:T(8,128)}, f32[8,2048]{0,1:T(8,128)}), (f32[2048,8]{1,0:T(8,128)}, f32[8,2048]{0,1:T(8,128)})) %all-reduce.10.cloned.1.call-update) | async-done | bytes 131088 | tf_op jit(solution)/shard_map/psum | solution.py:91
  551.5 3.8 gather_fusion.5
  555.3 1.1 fusion.9
  557.2 1.1 copy.160
  558.3 16.8 %all-to-all-start.6 = ((f32[128,12,8]{1,2,0:T(8,128)}), f32[128,12,8]{1,2,0:T(8,128)S(1)}, u32[]{:S(2)}, u32[]{:S(2)}) async-start(f32[128,12,8]{1,2,0:T(8,128)} %copy.160), calls=%async_computation.6 | async-start | bytes 1048576 | tf_op jit(solution)/shard_map/all_to_all | solution.py:92
  575.1 1.3 select_bitcast_fusion
  577.8 30.3 %all-to-all-done.6 = f32[128,12,8]{1,2,0:T(8,128)S(1)} async-done(((f32[128,12,8]{1,2,0:T(8,128)}), f32[128,12,8]{1,2,0:T(8,128)S(1)}, u32[]{:S(2)}, u32[]{:S(2)}) %all-to-all-start.6) | async-done | bytes 49184 | tf_op jit(solution)/shard_map/all_to_all | solution.py:92
  608.7 1.6 gather_fusion.2
  611.2 0.8 copy.168
  (131 shorter events, 19.7 us)
Async XLA Ops:
  7.2 233.7 %copy-start = (f32[40,40]{1,0:T(8,128)S(1)}, f32[40,40]{1,0:T(8,128)}, u32[]{:S(2)}) copy-start(f32[40,40]{1,0:T(8,128)} %param.21) | copy-start | bytes 19204
  7.2 1.2 copy-start.6
  7.2 1.3 copy-start.8
  7.2 25.1 %copy-start.1 = (f32[4,2,4,2,1024]{4,3,2,1,0:T(2,128)S(1)}, f32[4,2,4,2,1024]{4,3,2,1,0:T(2,128)}, u32[]{:S(2)}) copy-start(f32[4,2,4,2,1024]{4,3,2,1,0:T(2,128)} %param.18) | copy-start | bytes 786436
  8.4 29.5 %copy-start.2 = (f32[40,2,768]{2,1,0:T(2,128)S(1)}, f32[40,2,768]{2,1,0:T(2,128)}, u32[]{:S(2)}) copy-start(f32[40,2,768]{2,1,0:T(2,128)} %param.19) | copy-start | bytes 737284
  8.4 29.5 %copy-start.3 = (f32[4,40]{1,0:T(4,128)S(1)}, f32[4,40]{1,0:T(4,128)}, u32[]{:S(2)}) copy-start(f32[4,40]{1,0:T(4,128)} %param.22) | copy-start | bytes 1924
  8.4 29.8 %copy-start.4 = (f32[4,2,1024]{2,1,0:T(2,128)S(1)}, f32[4,2,1024]{2,1,0:T(2,128)}, u32[]{:S(2)}) copy-start(f32[4,2,1024]{2,1,0:T(2,128)} %param.20) | copy-start | bytes 98308
  8.5 233.2 %copy-start.5 = (s32[768]{0:T(1024)}, s32[768]{0:T(1024)S(1)}, u32[]{:S(2)}) copy-start(s32[768]{0:T(1024)S(1)} %fusion.59) | copy-start | bytes 9220
  12.6 33.5 %all-to-all-start = ((s32[128,1,12]{2,1,0:T(1,128)}), s32[128,1,12]{2,1,0:T(1,128)S(1)}, u32[]{:S(2)}, u32[]{:S(2)}) async-start(s32[128,1,12]{2,1,0:T(1,128)} %bitcast), calls=%async_computation | async-start | bytes 131072 | tf_op jit(solution)/shard_map/all_to_all | solution.py:65
  32.5 31.3 %collective-permute-start = (f32[4,2,4,1,1024]{4,3,1,0,2:T(1,128)S(1)}, f32[4,2,4,1,1024]{4,3,1,0,2:T(1,128)S(1)}, u32[]{:S(2)}, u32[]{:S(2)}) collective-permute-start(f32[4,2,4,1,1024]{4,3,1,0,2:T(1,128)S(1)} %get-tuple-element.80), channel_id=1, source_target_pairs={{0,4},{4,8},{8,12},{12,16},{16,20},{20,24},{24,28},{28,32},{32,36}... | collective-permute-start | bytes 393224 | tf_op jit(solution)/shard_map/ppermute | solution.py:21
  35.9 27.9 %collective-permute-start.1 = (f32[4,2,4,1,1024]{4,3,1,0,2:T(1,128)S(1)}, f32[4,2,4,1,1024]{4,3,1,0,2:T(1,128)S(1)}, u32[]{:S(2)}, u32[]{:S(2)}) collective-permute-start(f32[4,2,4,1,1024]{4,3,1,0,2:T(1,128)S(1)} %get-tuple-element.79), channel_id=1, source_target_pairs={{4,0},{8,4},{12,8},{16,12},{20,16},{24,20},{28,24},{32,28},{36,32}... | collective-permute-start | bytes 393224 | tf_op jit(solution)/shard_map/ppermute | solution.py:22
  46.1 50.2 %all-to-all-start.1 = ((f32[128,12,8]{1,2,0:T(8,128)}), f32[128,12,8]{1,2,0:T(8,128)S(1)}, u32[]{:S(2)}, u32[]{:S(2)}) async-start(f32[128,12,8]{1,2,0:T(8,128)} %copy.122), calls=%async_computation.1 | async-start | bytes 1048576 | tf_op jit(solution)/shard_map/all_to_all | solution.py:85
  63.4 109.6 %all-reduce.14.cloned.1.call-start = ((), (), s32[]{:S(2)}) async-start(), calls=%async_computation.9 | async-start | bytes 4194304 | tf_op jit(solution)/shard_map/psum | solution.py:91
  64.0 42.7 %collective-permute-start.2 = (f32[4,2,1,4,1024]{4,3,1,0,2:T(4,128)S(1)}, f32[4,2,1,4,1024]{4,3,1,0,2:T(4,128)S(1)}, u32[]{:S(2)}, u32[]{:S(2)}) collective-permute-start(f32[4,2,1,4,1024]{4,3,1,0,2:T(4,128)S(1)} %get-tuple-element.67), channel_id=1, source_target_pairs={{1,0},{2,1},{3,2},{5,4},{6,5},{7,6},{9,8},{10,9},{11,10},{13,12},{... | collective-permute-start | bytes 393224 | tf_op jit(solution)/shard_map/ppermute | solution.py:22
  65.3 41.4 %collective-permute-start.3 = (f32[4,2,1,4,1024]{4,3,1,0,2:T(4,128)S(1)}, f32[4,2,1,4,1024]{4,3,1,0,2:T(4,128)S(1)}, u32[]{:S(2)}, u32[]{:S(2)}) collective-permute-start(f32[4,2,1,4,1024]{4,3,1,0,2:T(4,128)S(1)} %get-tuple-element.68), channel_id=1, source_target_pairs={{0,1},{1,2},{2,3},{4,5},{5,6},{6,7},{8,9},{9,10},{10,11},{12,13},{... | collective-permute-start | bytes 393224 | tf_op jit(solution)/shard_map/ppermute | solution.py:21
  106.7 0.7 copy-start.7
  175.0 31.5 %collective-permute-start.4 = (f32[4,2,4,1,1024]{4,3,1,0,2:T(1,128)S(1)}, f32[4,2,4,1,1024]{4,3,1,0,2:T(1,128)S(1)}, u32[]{:S(2)}, u32[]{:S(2)}) collective-permute-start(f32[4,2,4,1,1024]{4,3,1,0,2:T(1,128)S(1)} %get-tuple-element.76), channel_id=1, source_target_pairs={{0,4},{4,8},{8,12},{12,16},{16,20},{20,24},{24,28},{28,32},{32,36}... | collective-permute-start | bytes 393224 | tf_op jit(solution)/shard_map/ppermute | solution.py:21
  178.7 27.8 %collective-permute-start.5 = (f32[4,2,4,1,1024]{4,3,1,0,2:T(1,128)S(1)}, f32[4,2,4,1,1024]{4,3,1,0,2:T(1,128)S(1)}, u32[]{:S(2)}, u32[]{:S(2)}) collective-permute-start(f32[4,2,4,1,1024]{4,3,1,0,2:T(1,128)S(1)} %get-tuple-element.75), channel_id=1, source_target_pairs={{4,0},{8,4},{12,8},{16,12},{20,16},{24,20},{28,24},{32,28},{36,32}... | collective-permute-start | bytes 393224 | tf_op jit(solution)/shard_map/ppermute | solution.py:22
  187.5 50.5 %all-to-all-start.2 = ((f32[128,12,8]{1,2,0:T(8,128)}), f32[128,12,8]{1,2,0:T(8,128)S(1)}, u32[]{:S(2)}, u32[]{:S(2)}) async-start(f32[128,12,8]{1,2,0:T(8,128)} %copy.130), calls=%async_computation.2 | async-start | bytes 1048576 | tf_op jit(solution)/shard_map/all_to_all | solution.py:92
  206.7 92.0 %collective-permute-start.6 = (f32[4,2,1,4,1024]{4,3,1,0,2:T(4,128)S(1)}, f32[4,2,1,4,1024]{4,3,1,0,2:T(4,128)S(1)}, u32[]{:S(2)}, u32[]{:S(2)}) collective-permute-start(f32[4,2,1,4,1024]{4,3,1,0,2:T(4,128)S(1)} %get-tuple-element.65), channel_id=1, source_target_pairs={{1,0},{2,1},{3,2},{5,4},{6,5},{7,6},{9,8},{10,9},{11,10},{13,12},{... | collective-permute-start | bytes 393224 | tf_op jit(solution)/shard_map/ppermute | solution.py:22
  208.0 90.7 %collective-permute-start.7 = (f32[4,2,1,4,1024]{4,3,1,0,2:T(4,128)S(1)}, f32[4,2,1,4,1024]{4,3,1,0,2:T(4,128)S(1)}, u32[]{:S(2)}, u32[]{:S(2)}) collective-permute-start(f32[4,2,1,4,1024]{4,3,1,0,2:T(4,128)S(1)} %get-tuple-element.66), channel_id=1, source_target_pairs={{0,1},{1,2},{2,3},{4,5},{5,6},{6,7},{8,9},{9,10},{10,11},{12,13},{... | collective-permute-start | bytes 393224 | tf_op jit(solution)/shard_map/ppermute | solution.py:21
  247.9 39.9 %all-to-all-start.3 = ((f32[128,12,8]{1,2,0:T(8,128)}), f32[128,12,8]{1,2,0:T(8,128)S(1)}, u32[]{:S(2)}, u32[]{:S(2)}) async-start(f32[128,12,8]{1,2,0:T(8,128)} %copy.138), calls=%async_computation.3 | async-start | bytes 1048576 | tf_op jit(solution)/shard_map/all_to_all | solution.py:85
  255.0 107.4 %all-reduce.12.cloned.1.call-start = ((), (), s32[]{:S(2)}) async-start(), calls=%async_computation.8 | async-start | bytes 4194304 | tf_op jit(solution)/shard_map/psum | solution.py:91
  371.1 49.7 %all-to-all-start.4 = ((f32[128,12,8]{1,2,0:T(8,128)}), f32[128,12,8]{1,2,0:T(8,128)S(1)}, u32[]{:S(2)}, u32[]{:S(2)}) async-start(f32[128,12,8]{1,2,0:T(8,128)} %copy.145), calls=%async_computation.4 | async-start | bytes 1048576 | tf_op jit(solution)/shard_map/all_to_all | solution.py:92
  388.1 20.1 %collective-permute-start.8 = (f32[4,2,4,1,1024]{4,3,1,0,2:T(1,128)S(1)}, f32[4,2,4,1,1024]{4,3,1,0,2:T(1,128)S(1)}, u32[]{:S(2)}, u32[]{:S(2)}) collective-permute-start(f32[4,2,4,1,1024]{4,3,1,0,2:T(1,128)S(1)} %get-tuple-element.72), channel_id=1, source_target_pairs={{0,4},{4,8},{8,12},{12,16},{16,20},{20,24},{24,28},{28,32},{32,36}... | collective-permute-start | bytes 393224 | tf_op jit(solution)/shard_map/ppermute | solution.py:21
  391.5 21.6 %collective-permute-start.9 = (f32[4,2,4,1,1024]{4,3,1,0,2:T(1,128)S(1)}, f32[4,2,4,1,1024]{4,3,1,0,2:T(1,128)S(1)}, u32[]{:S(2)}, u32[]{:S(2)}) collective-permute-start(f32[4,2,4,1,1024]{4,3,1,0,2:T(1,128)S(1)} %get-tuple-element.71), channel_id=1, source_target_pairs={{4,0},{8,4},{12,8},{16,12},{20,16},{24,20},{28,24},{32,28},{36,32}... | collective-permute-start | bytes 393224 | tf_op jit(solution)/shard_map/ppermute | solution.py:22
  413.2 74.6 %collective-permute-start.10 = (f32[4,2,1,4,1024]{4,3,1,0,2:T(4,128)S(1)}, f32[4,2,1,4,1024]{4,3,1,0,2:T(4,128)S(1)}, u32[]{:S(2)}, u32[]{:S(2)}) collective-permute-start(f32[4,2,1,4,1024]{4,3,1,0,2:T(4,128)S(1)} %get-tuple-element.63), channel_id=1, source_target_pairs={{1,0},{2,1},{3,2},{5,4},{6,5},{7,6},{9,8},{10,9},{11,10},{13,12},{... | collective-permute-start | bytes 393224 | tf_op jit(solution)/shard_map/ppermute | solution.py:22
  414.5 73.3 %collective-permute-start.11 = (f32[4,2,1,4,1024]{4,3,1,0,2:T(4,128)S(1)}, f32[4,2,1,4,1024]{4,3,1,0,2:T(4,128)S(1)}, u32[]{:S(2)}, u32[]{:S(2)}) collective-permute-start(f32[4,2,1,4,1024]{4,3,1,0,2:T(4,128)S(1)} %get-tuple-element.64), channel_id=1, source_target_pairs={{0,1},{1,2},{2,3},{4,5},{5,6},{6,7},{8,9},{9,10},{10,11},{12,13},{... | collective-permute-start | bytes 393224 | tf_op jit(solution)/shard_map/ppermute | solution.py:21
  430.9 46.6 %all-to-all-start.5 = ((f32[128,12,8]{1,2,0:T(8,128)}), f32[128,12,8]{1,2,0:T(8,128)S(1)}, u32[]{:S(2)}, u32[]{:S(2)}) async-start(f32[128,12,8]{1,2,0:T(8,128)} %copy.154), calls=%async_computation.5 | async-start | bytes 1048576 | tf_op jit(solution)/shard_map/all_to_all | solution.py:85
  444.5 107.0 %all-reduce.10.cloned.1.call-start = ((), (), s32[]{:S(2)}) async-start(), calls=%async_computation.7 | async-start | bytes 4194304 | tf_op jit(solution)/shard_map/psum | solution.py:91
  558.3 49.7 %all-to-all-start.6 = ((f32[128,12,8]{1,2,0:T(8,128)}), f32[128,12,8]{1,2,0:T(8,128)S(1)}, u32[]{:S(2)}, u32[]{:S(2)}) async-start(f32[128,12,8]{1,2,0:T(8,128)} %copy.160), calls=%async_computation.6 | async-start | bytes 1048576 | tf_op jit(solution)/shard_map/all_to_all | solution.py:92
Sparse Core Ops, SparseCore 0:
  106.9 66.0 all-reduce.13
  298.8 63.4 all-reduce.11
  488.0 63.4 all-reduce.9
where the time goes:
time: 627 us; the launch traced here: 619 us
  waiting for transfers between devices  357 us (57%)
  starting transfers between devices  141 us (22%)
  local copies, waits for them, and re-layouts  59.6 us (10%)
  other arithmetic  42.7 us (7%)
  between operations  14.9 us (2%)
    psum x3, waiting for transfers between devices, apply(): added = lax.psum(local_add, 'depth')  189 us
    all_to_all x3, waiting for transfers between devices, apply(): lax.all_to_all(sent, 'tile', split_axis=0, concat_axis=0, tiled=True)  91.3 us
    all_to_all x3, waiting for transfers between devices, apply(): lax.all_to_all(answer.reshape(tiles, capacity, width), 'tile', split_axis...  58.4 us
    all_to_all x3, starting transfers between devices, apply(): lax.all_to_all(answer.reshape(tiles, capacity, width), 'tile', split_axis...  51.2 us
    all_to_all x3, starting transfers between devices, apply(): lax.all_to_all(sent, 'tile', split_axis=0, concat_axis=0, tiled=True)  37.9 us
    scatter-add x3, other arithmetic, apply(): local_add = jnp.zeros((spots_n, width), jnp.float32).at[row_index].add(got)  29.7 us
    ppermute x6, starting transfers between devices, extended(): before = lax.ppermute(last, axis, up)  22.8 us
    all_to_all x1, starting transfers between devices, per_device(): lax.all_to_all(sent_spots, 'tile', split_axis=0, concat_axis=0, tiled=True)  19.7 us
  transfers between devices with their start and end apart: 22, of which 11 were waited for; matrix products, arithmetic and copies ran while one was open for 13% of the time, Pallas kernels for 0%

commit v1 on v0

v1 whole, which is shorter than its diff:
```python
import jax
import jax.numpy as jnp
from jax import lax
from jax.experimental import pallas as pl
from jax.experimental.pallas import tpu as pltpu
from jax.sharding import PartitionSpec as P

HOP = 0.12
MU = 0.15
PAIR = 0.3
CAP = 12
LANES = 32
EXACT = lax.Precision.HIGHEST
F32 = jnp.float32
BF16 = jnp.bfloat16


def iota(shape, dim):
    return lax.broadcasted_iota(jnp.int32, shape, dim)


def split(x):
    high = x.astype(BF16)
    return high, (x - high.astype(F32)).astype(BF16)


def dot(a, b):
    return jnp.dot(a, b, preferred_element_type=F32)


def dot3(a, b):
    return dot(a[0], b[0]) + dot(a[0], b[1]) + dot(a[1], b[0])


def dot_rows(a, b):
    return lax.dot_general(a, b, (((1,), (1,)), ((), ())), preferred_element_type=F32)


def beside(s):
    rank = s.ndim
    sub, lane = iota(s.shape, rank - 2), iota(s.shape, rank - 1)
    left = pltpu.roll(s, 1, rank - 1)
    left = jnp.where(lane == 0, pltpu.roll(left, 1, rank - 2), left)
    left = jnp.where((lane == 0) & (sub == 0), 0.0, left)
    right = pltpu.roll(s, 127, rank - 1)
    right = jnp.where(lane == 127, pltpu.roll(right, 7, rank - 2), right)
    right = jnp.where((lane == 127) & (sub == 7), 0.0, right)
    return left + right


def local_part(s, disorder, around):
    inner = (disorder - MU) * s - HOP * around
    return jnp.concatenate(
        [inner[:4] + PAIR * s[4:], PAIR * s[:4] - inner[4:]], axis=0
    )


def signed(s):
    return jnp.concatenate([s[:4], -s[4:]], axis=0)


def route_kernel(a_ref, tile_ref, spot_ref, block_ref, coup_ref, msg_ref, rank_ref):
    count = a_ref.shape[2]
    tiles = msg_ref.shape[0]
    a = split(jnp.concatenate([a_ref[0], a_ref[1]], axis=1))
    c, b = coup_ref[...], block_ref[...]
    cb = jnp.dot(c, b, precision=EXACT, preferred_element_type=F32)
    cbb = jnp.dot(cb, b, precision=EXACT, preferred_element_type=F32)
    w = jnp.concatenate([c, cb, cbb], axis=0)
    i, j = iota((24, 12), 0), iota((24, 12), 1)
    spread = (j == (i // 8) * 4 + (i % 8) // 2).astype(F32)
    w = split(jnp.dot(spread, w, precision=EXACT, preferred_element_type=F32))
    g = dot3(w, a)
    val = jnp.where(iota((24, count), 0) % 2 == 0, g[:, :count], g[:, count:])
    spot = spot_ref[...]
    row, col = spot >> 10, spot & 1023
    below = jnp.where(row == 0, col + 1025, 0)
    above = jnp.where(row == 1, col + 1, 0)
    vals = jnp.concatenate(
        [val, (spot + 1).astype(F32), below.astype(F32), above.astype(F32), jnp.zeros((5, count), F32)],
        axis=0,
    )
    hot = (iota((tiles, count), 0) == tile_ref[...]).astype(F32)
    hot16 = hot.astype(BF16)
    earlier = (iota((count, count), 0) < iota((count, count), 1)).astype(F32).astype(BF16)
    rank = jnp.sum(dot(hot16, earlier) * hot, axis=0, keepdims=True).astype(jnp.int32)
    rank_ref[...] = rank
    slots = split(
        jnp.concatenate([jnp.where(rank == r, vals, 0.0) for r in range(CAP)], axis=0)
    )
    msg = dot_rows(hot16, slots[0]) + dot_rows(hot16, slots[1])
    at, kind = iota(msg.shape, 0), iota(msg.shape, 1) % LANES
    up = jnp.where(at == tiles - 1, 0.0, pltpu.roll(msg, tiles - 1, 0))
    down = jnp.where(at == 0, 0.0, pltpu.roll(msg, 1, 0))
    msg_ref[:, 0, :] = jnp.where(kind == 25, up, jnp.where(kind == 26, down, msg))


def pure_kernel(pos_ref, x_ref, lo_ref, hi_ref, top_ref, one_ref, two_ref, s1_ref):
    first_layer = pos_ref[0] == 0
    last_layer = pos_ref[0] == pos_ref[1] - 1
    first_row = pos_ref[2] == 0
    last_row = pos_ref[2] == pos_ref[3] - 1

    def inside(l, r):
        out = None
        if l < 0:
            out = first_layer
        if l > 3:
            out = last_layer
        if r < 0:
            out = first_row if out is None else out | first_row
        if r > 1:
            out = last_row if out is None else out | last_row
        return out

    def masked(s, l, r):
        out = inside(l, r)
        return s if out is None else jnp.where(out, 0.0, s)

    def start(l, r):
        if r < 0:
            return lo_ref[:, l + 2, r + 2]
        if r > 1:
            return hi_ref[:, l + 2, r - 2]
        return x_ref[:, l + 3, r]

    def s0(l, r):
        return start(l, r)[:8]

    for l in range(-2, 6):
        for r in range(-1, 3):
            if r in (-1, 2) and l in (-2, 5):
                continue
            here = start(l, r)
            s = here[:8]
            around = beside(s) + s0(l - 1, r) + s0(l + 1, r) + s0(l, r - 1) + s0(l, r + 1)
            s1_ref[:, l + 2, r + 1] = masked(local_part(s, here[8:9], around), l, r)
    for l in range(-1, 5):
        for r in range(2):
            s = s1_ref[:, l + 2, r + 1]
            around = beside(s) + s1_ref[:, l + 1, r + 1] + s1_ref[:, l + 3, r + 1]
            around = around + s1_ref[:, l + 2, r] + s1_ref[:, l + 2, r + 2]
            new = 2.0 * local_part(s, x_ref[8:9, l + 3, r], around) - s0(l, r)
            two_ref[:, l + 1, r] = masked(new, l, r)
            if 0 <= l < 4:
                one_ref[:, l, r] = s
            if l == 0:
                rows = pl.ds(8 * r, 8)
                under = s1_ref[:, l + 3, r + 1]
                top_ref[0:8, rows, :] = s
                top_ref[8:16, rows, :] = -2.0 * HOP * signed(under) - s0(l, r)
                top_ref[16:25, rows, :] = start(l, r)
                top_ref[25:26, rows, :] = jnp.zeros((1, 8, 128), F32)


def columns(got):
    width = got.shape[1] // 128
    return jnp.concatenate([got[:, 128 * j : 128 * (j + 1)].T for j in range(width)], axis=0)


def scatter_kernel(pos_ref, got_ref, top_ref, out_ref, d2_ref, site_ref, dense_ref):
    got = got_ref[:, 0, :]
    tiles = got.shape[0]
    slots = columns(got)
    kind = iota((LANES, tiles), 0)
    lane = iota((tiles, 128), 1)
    for r in range(CAP):
        mine = slots[r * LANES : (r + 1) * LANES]
        sites = mine[24:27].astype(jnp.int32) - 1
        site_ref[r : r + 1] = sites[0:1]
        site_ref[16 + r : 17 + r] = sites[1:2]
        site_ref[32 + r : 33 + r] = sites[2:3]
        high = sites[0:1] >> 7
        vals = jnp.where(kind < 24, mine, jnp.where(kind == 24, 1.0, 0.0))
        near = vals.astype(BF16).astype(F32)
        rest = vals - near
        left = jnp.concatenate(
            [
                jnp.concatenate([jnp.where(high == h, part, 0.0) for h in range(16)], axis=0)
                for part in (near, rest)
            ],
            axis=1,
        ).astype(BF16)
        at = (got[:, r * LANES + 24 : r * LANES + 25].astype(jnp.int32) - 1) & 127
        right = (at == lane).astype(F32).astype(BF16)
        part = dot(left, jnp.concatenate([right, right], axis=0))
        dense_ref[...] = part if r == 0 else dense_ref[...] + part

    def dense(k):
        return dense_ref[pl.ds(k, 16, stride=LANES), :]

    on = pos_ref[0] == 0
    for k in range(8):
        q1 = dense(k) + jnp.where(on, top_ref[k], 0.0)
        q2 = 2.0 * dense(8 + k) + jnp.where(on, top_ref[8 + k], 0.0)
        d2 = dense(16 + k)
        d2_ref[k] = d2
        tail = jnp.where(on, top_ref[16 + k], d2)
        for y in range(4):
            out_ref[y, k] = q1
            out_ref[y, 8 + k] = q2
            out_ref[y, 16 + k] = tail
    number = dense(24)
    field = jnp.where(on, top_ref[24], 0.0)
    for y in range(4):
        out_ref[y, 24] = field
        out_ref[y, 25] = number


def evolve_kernel(
    pos_ref, m_ref, top_ref, d2_ref, site_ref, coup_ref, block_ref, two_ref,
    ans_ref, d_ref, low_ref, high_ref, f_ref, f1_ref,
):
    tiles = site_ref.shape[1]
    on = pos_ref[0] == 0
    c = coup_ref[...]
    cb = jnp.dot(c, block_ref[...], precision=EXACT, preferred_element_type=F32)
    nt = (((1,), (1,)), ((), ()))
    kk = lax.dot_general(c, c, nt, precision=EXACT, preferred_element_type=F32)
    kb = lax.dot_general(cb, c, nt, precision=EXACT, preferred_element_type=F32)

    def mix(k, s):
        def row(o):
            terms = [k[o : o + 1, q : q + 1] * s[2 * q : 2 * q + 2] for q in range(4)]
            return (terms[0] + terms[1]) + (terms[2] + terms[3])

        return jnp.concatenate([row(o) for o in range(4)], axis=0)

    def rows_of(s):
        return s.reshape(s.shape[0], 2, 8, 128)

    s0 = m_ref[0, 16:24]
    field = rows_of(m_ref[0, 24:25])
    s1 = (m_ref[0, 0:8] + m_ref[1, 0:8]) + (m_ref[2, 0:8] + m_ref[3, 0:8])
    q2 = (m_ref[0, 8:16] + m_ref[1, 8:16]) + (m_ref[2, 8:16] + m_ref[3, 8:16])
    number = (m_ref[0, 25:26] + m_ref[1, 25:26]) + (m_ref[2, 25:26] + m_ref[3, 25:26])

    def flat_part(s):
        s = rows_of(s)
        other = jnp.concatenate([s[:, 1:2], s[:, 0:1]], axis=1)
        return local_part(s, field, beside(s) + other).reshape(8, 16, 128)

    hopped = q2 + 2.0 * (number * mix(kk, s0))
    s2 = hopped + 2.0 * flat_part(s1)
    d0 = jnp.where(on, s1 - top_ref[0:8], 0.0)
    delta = jnp.where(on, hopped - top_ref[8:16] + 2.0 * flat_part(d0), 0.0)
    d2 = d2_ref[...] + (m_ref[1, 16:24] + m_ref[2, 16:24] + m_ref[3, 16:24])
    third = 2.0 * (d2 + number * (mix(kb, s0) + mix(kk, s1))) - d0
    d_ref[0:8] = d0
    d_ref[8:16] = delta
    d_ref[16:24] = jnp.where(on, third, 0.0)
    hop0 = -2.0 * HOP * signed(rows_of(d0))
    d0r, deltar = rows_of(d0), rows_of(delta)
    for r, ref in ((0, low_ref), (1, high_ref)):
        ref[:, 0] = two_ref[:, 1, r] + deltar[:, r]
        ref[:, 1] = two_ref[:, 2, r] + hop0[:, r]
        ref[:, 2] = two_ref[:, 3, r]
        ref[:, 3] = two_ref[:, 4, r]
        ref[:, 4] = d0r[:, r]

    for k in range(8):
        f_ref[pl.ds(k, 16, stride=24), :] = s0[k]
        f_ref[pl.ds(8 + k, 16, stride=24), :] = s1[k]
        f_ref[pl.ds(16 + k, 16, stride=24), :] = s2[k]
        f1_ref[pl.ds(k, 16, stride=8), :] = s1[k]
    f = jnp.concatenate(split(f_ref[...]), axis=1)
    f1 = jnp.concatenate(split(f1_ref[...]), axis=1)
    sub = iota((128, 2 * tiles), 0)

    def pick(table, width, sites):
        right = (sub == (sites & 127)).astype(F32).astype(BF16)
        found = dot(table, jnp.concatenate([right, right], axis=0))
        high = sites >> 7
        out = jnp.zeros((width, sites.shape[1]), F32)
        for h in range(16):
            out = out + jnp.where(high == h, found[h * width : (h + 1) * width], 0.0)
        return out

    own, low, high = [], [], []
    for r in range(0, CAP, 2):
        for table, width, base, out in ((f, 24, 0, own), (f1, 8, 16, low), (f1, 8, 32, high)):
            sites = jnp.concatenate(
                [site_ref[base + r : base + r + 1], site_ref[base + r + 1 : base + r + 2]], axis=1
            )
            both = pick(table, width, sites)
            out += [both[:, :tiles], both[:, tiles:]]
    answer = jnp.concatenate(own + low + high + [jnp.zeros((32, tiles), F32)], axis=0)
    for j in range(4):
        ans_ref[:, j, :] = answer[128 * j : 128 * (j + 1)].T


def adatom_kernel(a_ref, back_ref, tile_ref, rank_ref, block_ref, coup_ref, prev_ref, last_ref):
    count = a_ref.shape[2]
    tiles = back_ref.shape[0]
    back = jnp.concatenate([back_ref[:, j, :].T for j in range(4)], axis=0)
    back = jnp.concatenate(
        [back[:288], pltpu.roll(back[288:384], 1, 1), pltpu.roll(back[384:480], tiles - 1, 1)], axis=0
    )
    hot = (iota((tiles, count), 0) == tile_ref[...]).astype(F32).astype(BF16)
    found = dot(jnp.concatenate(split(back), axis=1), jnp.concatenate([hot, hot], axis=0))
    rank = rank_ref[...]
    s = jnp.zeros((24, count), F32)
    halo = jnp.zeros((8, count), F32)
    for r in range(CAP):
        here = rank == r
        s = s + jnp.where(here, found[24 * r : 24 * r + 24], 0.0)
        near = found[288 + 8 * r : 296 + 8 * r] + found[384 + 8 * r : 392 + 8 * r]
        halo = halo + jnp.where(here, near, 0.0)
    sign = jnp.where(iota((8, count), 0) < 4, 1.0, -1.0)
    s2 = s[16:24] - 2.0 * HOP * sign * halo
    b = split(block_ref[...])
    i, j = iota((4, 8), 0), iota((4, 8), 1)
    spread = (i == j // 2).astype(F32)
    c = split(
        lax.dot_general(
            coup_ref[...], spread, (((0,), (0,)), ((), ())), precision=EXACT, preferred_element_type=F32
        )
    )
    even = iota((8, count), 0) % 2 == 0

    def apply(a, s):
        s = jnp.concatenate([jnp.where(even, s, 0.0), jnp.where(even, 0.0, s)], axis=1)
        return dot3(b, split(a)) + dot3(c, split(s))

    a0 = jnp.concatenate([a_ref[0], a_ref[1]], axis=1)
    a1 = apply(a0, s[0:8])
    a2 = 2.0 * apply(a1, s[8:16]) - a0
    a3 = 2.0 * apply(a2, s2) - a1
    for v in range(2):
        prev_ref[v] = a2[:, v * count : (v + 1) * count]
        last_ref[v] = a3[:, v * count : (v + 1) * count]


def last_kernel(pos_ref, x_ref, one_ref, two_ref, d_ref, before_ref, after_ref, prev_ref, last_ref):
    has_before = pos_ref[2] > 0
    has_after = pos_ref[2] < pos_ref[3] - 1
    d0 = d_ref[0:8].reshape(8, 2, 8, 128)
    delta = d_ref[8:16].reshape(8, 2, 8, 128)
    third = d_ref[16:24].reshape(8, 2, 8, 128)

    def hop(s):
        return -2.0 * HOP * signed(s)

    hop0 = [hop(d0[:, r]) for r in range(2)]
    for r, ref in ((0, before_ref), (1, after_ref)):
        prev_ref[:, 0, r] = two_ref[:, 1, r] + delta[:, r] + hop(ref[:, 4])
        prev_ref[:, 1, r] = two_ref[:, 2, r] + hop0[r]
        prev_ref[:, 2, r] = two_ref[:, 3, r]
        prev_ref[:, 3, r] = two_ref[:, 4, r]

    def beyond(l, r):
        ref, there = (before_ref, has_before) if r == 0 else (after_ref, has_after)
        s = ref[:, l]
        if l == 0:
            s = s + jnp.where(there, hop0[r], 0.0)
        return s

    for l in range(4):
        for r in range(2):
            s = prev_ref[:, l, r]
            over = two_ref[:, 0, r] if l == 0 else prev_ref[:, l - 1, r]
            under = two_ref[:, 5, r] if l == 3 else prev_ref[:, l + 1, r]
            around = beside(s) + over + under + prev_ref[:, l, 1 - r] + beyond(l, r)
            new = 2.0 * local_part(s, x_ref[8:9, l + 3, r], around) - one_ref[:, l, r]
            if l == 0:
                new = new + 2.0 * third[:, r] - d0[:, r]
            last_ref[:, l, r] = new


VM = pl.BlockSpec(memory_space=pltpu.VMEM)
SM = pl.BlockSpec(memory_space=pltpu.SMEM)


def shape(*dims, dtype=F32):
    return jax.ShapeDtypeStruct(dims, dtype)


def call(kernel, name, outs, args, scratch=(), smem=False, cost=100_000):
    return pl.pallas_call(
        kernel,
        out_shape=outs,
        in_specs=[SM if smem and i == 0 else VM for i in range(len(args))],
        out_specs=[VM] * len(outs),
        scratch_shapes=list(scratch),
        name=name,
        cost_estimate=pl.CostEstimate(flops=cost, bytes_accessed=1_000_000, transcendentals=0),
        compiler_params=pltpu.CompilerParams(vmem_limit_bytes=40 * 2**20),
    )(*args)


def per_device(
    substrate_start, adatom_start, disorder, adatom_block, coupling, adatom_tile, adatom_spot
):
    tiles, depths = lax.axis_size("tile"), lax.axis_size("depth")
    t, y = lax.axis_index("tile"), lax.axis_index("depth")
    count = adatom_spot.shape[0]
    pos = jnp.stack([y, jnp.int32(depths), t, jnp.int32(tiles)])

    def shifted(x, axis, size, step):
        pairs = [(i, i + step) for i in range(size) if 0 <= i + step < size]
        return lax.ppermute(x, axis, pairs)

    x = jnp.concatenate(
        [substrate_start.reshape(8, 4, 2, 8, 128), disorder.reshape(1, 4, 2, 8, 128)], axis=0
    )
    above = shifted(x[:, 1:], "depth", depths, 1)
    below = shifted(x[:, :3], "depth", depths, -1)

    a = adatom_start.transpose(1, 0, 2)
    own_tile = adatom_tile.reshape(1, count)
    msg, rank = call(
        route_kernel, "route",
        (shape(tiles, 1, CAP * LANES), shape(1, count, dtype=jnp.int32)),
        (a, own_tile, adatom_spot.reshape(1, count), adatom_block, coupling),
    )
    got = lax.all_to_all(msg, "tile", split_axis=0, concat_axis=0, tiled=True)

    x = jnp.concatenate([above, x, below], axis=1)
    lo = shifted(x[:, 1:9], "tile", tiles, 1)
    hi = shifted(x[:, 1:9], "tile", tiles, -1)
    top, one, two = call(
        pure_kernel, "pure",
        (shape(26, 16, 128), shape(8, 4, 2, 8, 128), shape(8, 6, 2, 8, 128)),
        (pos, x, lo, hi),
        (pltpu.VMEM((8, 8, 4, 8, 128), F32),), smem=True,
    )
    part, d2, site = call(
        scatter_kernel, "scatter",
        (shape(4, 26, 16, 128), shape(8, 16, 128), shape(48, tiles, dtype=jnp.int32)),
        (pos, got, top),
        (pltpu.VMEM((16 * LANES, 128), F32),), smem=True,
    )
    part = lax.all_to_all(part, "depth", split_axis=0, concat_axis=0, tiled=True)
    answer, d, low, high = call(
        evolve_kernel, "evolve",
        (shape(tiles, 4, 128), shape(24, 16, 128), shape(8, 5, 8, 128), shape(8, 5, 8, 128)),
        (pos, part, top, d2, site, coupling, adatom_block, two),
        (pltpu.VMEM((384, 128), F32), pltpu.VMEM((128, 128), F32)), smem=True,
    )
    before = shifted(high, "tile", tiles, 1)
    after = shifted(low, "tile", tiles, -1)
    back = lax.all_to_all(answer, "tile", split_axis=0, concat_axis=0, tiled=True)
    sub_prev, sub_last = call(
        last_kernel, "last",
        (shape(8, 4, 2, 8, 128), shape(8, 4, 2, 8, 128)),
        (pos, x, one, two, d, before, after), smem=True,
    )
    ad_prev, ad_last = call(
        adatom_kernel, "adatoms",
        (shape(2, 40, count), shape(2, 40, count)),
        (a, back, own_tile, rank, adatom_block, coupling),
    )
    return (
        sub_prev.reshape(4, 2, 4, 2, 1024),
        sub_last.reshape(4, 2, 4, 2, 1024),
        ad_prev.transpose(1, 0, 2),
        ad_last.transpose(1, 0, 2),
    )


def solution(mesh):
    in_specs = (
        P(None, None, "depth", "tile", None),
        P(None, None, ("tile", "depth")),
        P("depth", "tile", None),
        P(),
        P(),
        P(("tile", "depth"), None),
        P(("tile", "depth")),
    )
    out_specs = (
        P(None, None, "depth", "tile", None),
        P(None, None, "depth", "tile", None),
        P(None, None, ("tile", "depth")),
        P(None, None, ("tile", "depth")),
    )
    return jax.shard_map(
        per_device, mesh=mesh, in_specs=in_specs, out_specs=out_specs, check_vma=False
    )
```

time: 627 us -> 114 us (0.18); the launches traced: 619 us -> 113 us
  waiting for transfers between devices: 357 us -> 23.8 us
  starting transfers between devices: 141 us -> 52.3 us
  local copies, waits for them, and re-layouts: 59.6 us -> 6.07 us
  other arithmetic: 42.7 us -> 0.14 us
  blocking collectives: 0 us -> 17.5 us
  between operations: 14.9 us -> 0.87 us
  Pallas kernels: 0 us -> 12.4 us
    psum x3 -> x0, waiting for transfers between devices: 189 us -> none  [apply(): added = lax.psum(local_add, 'depth')]
    all_to_all x7 -> x2, waiting for transfers between devices: 150 us -> 6 us  [the longest x1 5.04 us: per_device(): lax.all_to_all(answer, 'tile', split_axis=0, concat_axis=0, tiled=True)]
    all_to_all x7 -> x2, starting transfers between devices: 109 us -> 34.8 us  [the longest x1 20 us: per_device(): got = lax.all_to_all(msg, 'tile', split_axis=0, concat_axis=0, tiled=True)]
    scatter-add x5 -> x0, other arithmetic: 29.8 us -> none  [the longest x3 29.7 us: apply(): local_add = jnp.zeros((spots_n, width), jnp.float32).at[row_index].add(got)]
    all_to_all x0 -> x1, blocking collectives: none -> 17.5 us  [per_device(): lax.all_to_all(part, 'depth', split_axis=0, concat_axis=0, tiled=True)]
    scatter x7 -> x0, local copies, waits for them, and re-layouts: 17.3 us -> none  [the longest x6 13.9 us: apply(): sent = jnp.zeros((slots_n, width), jnp.float32).at[slot].set(contrib).res...]
    gather x6 -> x0, local copies, waits for them, and re-layouts: 16.2 us -> none  [the longest x3 11.4 us: apply(): answer = jnp.take(shared, row_index, axis=1).T * live[:, None]]
    ppermute x12 -> x6, starting transfers between devices: 32.4 us -> 17.6 us  [shifted(): return lax.ppermute(x, axis, pairs)]
  transfers between devices with their start and end apart: 22 -> 8, of which waited for: 11 -> 5; matrix products, arithmetic and copies ran while one was open for 13% -> 2% of each run, Pallas kernels for 0% -> 4%
where the time goes in v1:
time: 114 us; the launch traced here: 113 us
  starting transfers between devices  52.3 us (46%)
  waiting for transfers between devices  23.8 us (21%)
  blocking collectives  17.5 us (15%)
  Pallas kernels  12.4 us (11%)
  local copies, waits for them, and re-layouts  6.07 us (5%)
    all_to_all x1, starting transfers between devices, per_device(): got = lax.all_to_all(msg, 'tile', split_axis=0, concat_axis=0, tiled=True)  20 us
    ppermute x6, waiting for transfers between devices, shifted(): return lax.ppermute(x, axis, pairs)  17.8 us
    ppermute x6, starting transfers between devices, shifted(): return lax.ppermute(x, axis, pairs)  17.6 us
    all_to_all x1, blocking collectives, per_device(): lax.all_to_all(part, 'depth', split_axis=0, concat_axis=0, tiled=True)  17.5 us
    all_to_all x1, starting transfers between devices, per_device(): lax.all_to_all(answer, 'tile', split_axis=0, concat_axis=0, tiled=True)  14.8 us
    pallas_call x6, Pallas kernels, call(): pl.pallas_call(kernel, out_shape=outs, in_specs=[SM if smem and i == 0 el...  12.4 us
    all_to_all x1, waiting for transfers between devices, per_device(): lax.all_to_all(answer, 'tile', split_axis=0, concat_axis=0, tiled=True)  5.04 us
    unnamed x14, local copies, waits for them, and re-layouts  2.37 us
  transfers between devices with their start and end apart: 8, of which 5 were waited for; matrix products, arithmetic and copies ran while one was open for 2% of the time, Pallas kernels for 4%

profile of v1, /device:TPU:7, one launch (start us, length us, event | category | flops | bytes accessed | tf_op | source)
XLA Modules:
  0.0 113.0 jit_solution(5639112854226192617)
XLA Ops:
  0.6 0.8 reshape.27
  1.4 1.2 %reshape.26 = f32[8,4,2,8,128]{4,3,2,1,0:T(8,128)S(1)} reshape(f32[4,2,4,2,1024]{4,3,2,1,0:T(2,128)} %param.7) | data formatting | bytes 524288 | tf_op jit(solution)/shard_map/reshape | solution.py:404
  2.6 0.0 copy-start.4
  2.6 0.0 copy-start.3
  2.7 3.3 %collective-permute-start = (f32[9,3,2,8,128]{4,3,2,1,0:T(8,128)S(1)}, f32[9,3,2,8,128]{4,3,2,1,0:T(8,128)S(1)}, u32[]{:S(2)}, u32[]{:S(2)}) collective-permute-start(f32[9,3,2,8,128]{4,3,2,1,0:T(8,128)S(1)} %get-tuple-element.40), channel_id=1, source_target_pairs={{0,1},{1,2},{2,3},{4,5},{5,6},{6,7},{8,9},{9,10},{10,11},{12,13},{... | collective-permute-start | bytes 663560 | tf_op jit(solution)/shard_map/ppermute | solution.py:401
  6.0 1.3 %collective-permute-start.1 = (f32[9,3,2,8,128]{4,3,2,1,0:T(8,128)S(1)}, f32[9,3,2,8,128]{4,3,2,1,0:T(8,128)S(1)}, u32[]{:S(2)}, u32[]{:S(2)}) collective-permute-start(f32[9,3,2,8,128]{4,3,2,1,0:T(8,128)S(1)} %get-tuple-element.41), channel_id=1, source_target_pairs={{1,0},{2,1},{3,2},{5,4},{6,5},{7,6},{9,8},{10,9},{11,10},{13,12},{... | collective-permute-start | bytes 663560 | tf_op jit(solution)/shard_map/ppermute | solution.py:401
  7.3 0.0 copy-done.4
  7.4 0.0 copy-done.3
  7.4 0.0 copy-start
  7.4 0.0 copy-start.2
  7.4 0.0 copy-start.1
  7.4 0.7 copy-done
  8.1 0.0 copy-done.2
  8.1 0.0 copy-done.1
  8.1 2.1 %route.1 = (f32[128,1,384]{2,1,0:T(1,128)}, s32[1,768]{1,0:T(1,128)S(1)}) custom-call(f32[2,40,768]{2,1,0:T(8,128)S(1)} %bitcast.12, s32[1,768]{1,0:T(1,128)S(1)} %bitcast.16, s32[1,768]{1,0:T(1,128)S(1)} %reshape.29.spot_ref, f32[40,40]{1,0:T(8,128)S(1)} %copy-done, f32[4,40]{1,0:T(4,128)S(1)} %copy-done.1), custom_call_target="tpu_custom_call" | custom-call | flops 100000 | bytes 1000000 | tf_op jit(solution)/shard_map/route/pallas_call | solution.py:379
  10.2 20.0 %all-to-all-start = ((f32[128,1,384]{2,1,0:T(1,128)}), f32[128,1,384]{2,1,0:T(1,128)S(1)}, u32[]{:S(2)}, u32[]{:S(2)}) async-start(f32[128,1,384]{2,1,0:T(1,128)} %get-tuple-element.22), calls=%async_computation | async-start | bytes 393216 | tf_op jit(solution)/shard_map/all_to_all | solution.py:416
  30.2 0.0 collective-permute-done
  30.2 0.0 collective-permute-done.1
  30.2 0.1 pad_maximum_fusion.x_ref
  30.3 2.3 %collective-permute-start.3 = (f32[9,8,2,8,128]{4,3,2,1,0:T(8,128)S(1)}, f32[9,8,2,8,128]{4,3,2,1,0:T(8,128)S(1)}, u32[]{:S(2)}, u32[]{:S(2)}) collective-permute-start(f32[9,8,2,8,128]{4,3,2,1,0:T(8,128)S(1)} %slice.15), channel_id=1, source_target_pairs={{4,0},{8,4},{12,8},{16,12},{20,16},{24,20},{28,24},{32,28},{36,32}... | collective-permute-start | bytes 1769480 | tf_op jit(solution)/shard_map/ppermute | solution.py:401
  32.6 5.4 %collective-permute-start.2 = (f32[9,8,2,8,128]{4,3,2,1,0:T(8,128)S(1)}, f32[9,8,2,8,128]{4,3,2,1,0:T(8,128)S(1)}, u32[]{:S(2)}, u32[]{:S(2)}) collective-permute-start(f32[9,8,2,8,128]{4,3,2,1,0:T(8,128)S(1)} %slice.15), channel_id=1, source_target_pairs={{0,4},{4,8},{8,12},{12,16},{16,20},{20,24},{24,28},{28,32},{32,36}... | collective-permute-start | bytes 1769480 | tf_op jit(solution)/shard_map/ppermute | solution.py:401
  38.0 0.1 pad_add_fusion.pos_ref
  38.1 8.7 %collective-permute-done.3.hi_ref = f32[9,8,2,8,128]{4,3,2,1,0:T(8,128)S(1)} collective-permute-done((f32[9,8,2,8,128]{4,3,2,1,0:T(8,128)S(1)}, f32[9,8,2,8,128]{4,3,2,1,0:T(8,128)S(1)}, u32[]{:S(2)}, u32[]{:S(2)}) %collective-permute-start.3) | collective-permute-done | bytes 589856 | tf_op jit(solution)/shard_map/ppermute | solution.py:401
  46.8 0.0 collective-permute-done.2.lo_ref
  46.8 1.4 %pure.1 = (f32[26,16,128]{2,1,0:T(8,128)S(1)}, f32[8,4,2,8,128]{4,3,2,1,0:T(8,128)S(1)}, f32[8,6,2,8,128]{4,3,2,1,0:T(8,128)S(1)}) custom-call(s32[4]{0:T(128)S(1)} %pad_add_fusion.pos_ref, f32[9,10,2,8,128]{4,3,2,1,0:T(8,128)S(1)} %pad_maximum_fusion.x_ref, f32[9,8,2,8,128]{4,3,2,1,0:T(8,128)S(1)} %collective-permute-done.2.lo_ref, ...), custom_call_target="tpu_custom_call" | custom-call | flops 100000 | bytes 1000000 | tf_op jit(solution)/shard_map/pure/pallas_call | solution.py:379
  48.2 1.0 all-to-all-done.got_ref
  49.2 3.3 %scatter.1 = (f32[4,26,16,128]{3,2,1,0:T(8,128)S(1)}, f32[8,16,128]{2,1,0:T(8,128)S(1)}, s32[48,128]{1,0:T(8,128)S(1)}) custom-call(s32[4]{0:T(128)S(1)} %pad_add_fusion.pos_ref, f32[128,1,384]{2,1,0:T(1,128)S(1)} %all-to-all-done.got_ref, f32[26,16,128]{2,1,0:T(8,128)S(1)} %get-tuple-element.23.top_ref), custom_call_target="tpu_custom_call" | custom-call | flops 100000 | bytes 1000000 | tf_op jit(solution)/shard_map/scatter/pallas_call | solution.py:379
  52.4 17.5 %all_to_all.15.m_ref = f32[4,26,16,128]{3,2,1,0:T(8,128)S(1)} all-to-all(f32[4,26,16,128]{3,2,1,0:T(8,128)S(1)} %get-tuple-element.24), channel_id=1, replica_groups=mesh['tile'=128,'depth'=4] {'depth'}, dimensions={0} | all-to-all | bytes 1703936 | tf_op jit(solution)/shard_map/all_to_all | solution.py:433
  69.9 2.8 %evolve.1 = (f32[128,4,128]{2,1,0:T(4,128)}, f32[24,16,128]{2,1,0:T(8,128)S(1)}, f32[8,5,8,128]{3,2,1,0:T(8,128)S(1)}, f32[8,5,8,128]{3,2,1,0:T(8,128)S(1)}) custom-call(s32[4]{0:T(128)S(1)} %pad_add_fusion.pos_ref, f32[4,26,16,128]{3,2,1,0:T(8,128)S(1)} %all_to_all.15.m_ref, f32[26,16,128]{2,1,0:T(8,128)S(1)} %get-tuple-element.23.top_ref, ...), custom_call_target="tpu_custom_call" | custom-call | flops 100000 | bytes 1000000 | tf_op jit(solution)/shard_map/evolve/pallas_call | solution.py:379
  72.7 14.8 %all-to-all-start.2 = ((f32[128,4,128]{2,1,0:T(4,128)}), f32[128,4,128]{2,1,0:T(4,128)S(1)}, u32[]{:S(2)}, u32[]{:S(2)}) async-start(f32[128,4,128]{2,1,0:T(4,128)} %get-tuple-element.32), calls=%async_computation.2 | async-start | bytes 524288 | tf_op jit(solution)/shard_map/all_to_all | solution.py:442
  87.5 3.3 %collective-permute-start.4 = (f32[8,5,8,128]{3,2,1,0:T(8,128)S(1)}, f32[8,5,8,128]{3,2,1,0:T(8,128)S(1)}, u32[]{:S(2)}, u32[]{:S(2)}) collective-permute-start(f32[8,5,8,128]{3,2,1,0:T(8,128)S(1)} %get-tuple-element.28), channel_id=1, source_target_pairs={{0,4},{4,8},{8,12},{12,16},{16,20},{20,24},{24,28},{28,32},{32,36}... | collective-permute-start | bytes 491528 | tf_op jit(solution)/shard_map/ppermute | solution.py:401
  90.8 1.9 %collective-permute-start.5 = (f32[8,5,8,128]{3,2,1,0:T(8,128)S(1)}, f32[8,5,8,128]{3,2,1,0:T(8,128)S(1)}, u32[]{:S(2)}, u32[]{:S(2)}) collective-permute-start(f32[8,5,8,128]{3,2,1,0:T(8,128)S(1)} %get-tuple-element.29), channel_id=1, source_target_pairs={{4,0},{8,4},{12,8},{16,12},{20,16},{24,20},{28,24},{32,28},{36,32}... | collective-permute-start | bytes 491528 | tf_op jit(solution)/shard_map/ppermute | solution.py:401
  92.8 6.1 %collective-permute-done.4.before_ref = f32[8,5,8,128]{3,2,1,0:T(8,128)S(1)} collective-permute-done((f32[8,5,8,128]{3,2,1,0:T(8,128)S(1)}, f32[8,5,8,128]{3,2,1,0:T(8,128)S(1)}, u32[]{:S(2)}, u32[]{:S(2)}) %collective-permute-start.4) | collective-permute-done | bytes 163872 | tf_op jit(solution)/shard_map/ppermute | solution.py:401
  98.9 3.0 %collective-permute-done.5.after_ref = f32[8,5,8,128]{3,2,1,0:T(8,128)S(1)} collective-permute-done((f32[8,5,8,128]{3,2,1,0:T(8,128)S(1)}, f32[8,5,8,128]{3,2,1,0:T(8,128)S(1)}, u32[]{:S(2)}, u32[]{:S(2)}) %collective-permute-start.5) | collective-permute-done | bytes 163872 | tf_op jit(solution)/shard_map/ppermute | solution.py:401
  101.9 0.8 last.1
  102.7 0.8 reshape.30
  103.5 0.8 reshape.31
  104.3 5.0 %all-to-all-done.2.back_ref = f32[128,4,128]{2,1,0:T(4,128)S(1)} async-done(((f32[128,4,128]{2,1,0:T(4,128)}), f32[128,4,128]{2,1,0:T(4,128)S(1)}, u32[]{:S(2)}, u32[]{:S(2)}) %all-to-all-start.2) | async-done | bytes 262176 | tf_op jit(solution)/shard_map/all_to_all | solution.py:442
  109.4 2.0 %adatoms.1 = (f32[2,40,768]{2,1,0:T(8,128)S(1)}, f32[2,40,768]{2,1,0:T(8,128)S(1)}) custom-call(f32[2,40,768]{2,1,0:T(8,128)S(1)} %bitcast.13, f32[128,4,128]{2,1,0:T(4,128)S(1)} %all-to-all-done.2.back_ref, s32[1,768]{1,0:T(1,128)S(1)} %bitcast.17, s32[1,768]{1,0:T(1,128)S(1)} %get-tuple-element.33.rank_ref, f32[40,40]{1,0:T(8,128)S(1)} %copy-done, ...), custom_call_target="tpu_custom_call" | custom-call | flops 100000 | bytes 1000000 | tf_op jit(solution)/shard_map/adatoms/pallas_call | solution.py:379
  111.4 0.8 copy.12
  112.2 0.8 copy.13
  (6 shorter events, 0.1 us)
Async XLA Ops:
  2.6 4.7 %copy-start.4 = (s32[768]{0:T(1024)S(1)}, s32[768]{0:T(1024)}, u32[]{:S(2)}) copy-start(s32[768]{0:T(1024)} %param.13) | copy-start | bytes 9220
  2.6 4.7 %copy-start.3 = (f32[40,2,768]{2,1,0:T(2,128)S(1)}, f32[40,2,768]{2,1,0:T(2,128)}, u32[]{:S(2)}) copy-start(f32[40,2,768]{2,1,0:T(2,128)} %param.8) | copy-start | bytes 737284
  2.7 27.5 %collective-permute-start = (f32[9,3,2,8,128]{4,3,2,1,0:T(8,128)S(1)}, f32[9,3,2,8,128]{4,3,2,1,0:T(8,128)S(1)}, u32[]{:S(2)}, u32[]{:S(2)}) collective-permute-start(f32[9,3,2,8,128]{4,3,2,1,0:T(8,128)S(1)} %get-tuple-element.40), channel_id=1, source_target_pairs={{0,1},{1,2},{2,3},{4,5},{5,6},{6,7},{8,9},{9,10},{10,11},{12,13},{... | collective-permute-start | bytes 663560 | tf_op jit(solution)/shard_map/ppermute | solution.py:401
  6.0 24.1 %collective-permute-start.1 = (f32[9,3,2,8,128]{4,3,2,1,0:T(8,128)S(1)}, f32[9,3,2,8,128]{4,3,2,1,0:T(8,128)S(1)}, u32[]{:S(2)}, u32[]{:S(2)}) collective-permute-start(f32[9,3,2,8,128]{4,3,2,1,0:T(8,128)S(1)} %get-tuple-element.41), channel_id=1, source_target_pairs={{1,0},{2,1},{3,2},{5,4},{6,5},{7,6},{9,8},{10,9},{11,10},{13,12},{... | collective-permute-start | bytes 663560 | tf_op jit(solution)/shard_map/ppermute | solution.py:401
  7.4 0.7 copy-start
  7.4 0.7 copy-start.2
  7.4 0.7 copy-start.1
  10.2 39.0 %all-to-all-start = ((f32[128,1,384]{2,1,0:T(1,128)}), f32[128,1,384]{2,1,0:T(1,128)S(1)}, u32[]{:S(2)}, u32[]{:S(2)}) async-start(f32[128,1,384]{2,1,0:T(1,128)} %get-tuple-element.22), calls=%async_computation | async-start | bytes 393216 | tf_op jit(solution)/shard_map/all_to_all | solution.py:416
  30.3 16.5 %collective-permute-start.3 = (f32[9,8,2,8,128]{4,3,2,1,0:T(8,128)S(1)}, f32[9,8,2,8,128]{4,3,2,1,0:T(8,128)S(1)}, u32[]{:S(2)}, u32[]{:S(2)}) collective-permute-start(f32[9,8,2,8,128]{4,3,2,1,0:T(8,128)S(1)} %slice.15), channel_id=1, source_target_pairs={{4,0},{8,4},{12,8},{16,12},{20,16},{24,20},{28,24},{32,28},{36,32}... | collective-permute-start | bytes 1769480 | tf_op jit(solution)/shard_map/ppermute | solution.py:401
  32.6 14.2 %collective-permute-start.2 = (f32[9,8,2,8,128]{4,3,2,1,0:T(8,128)S(1)}, f32[9,8,2,8,128]{4,3,2,1,0:T(8,128)S(1)}, u32[]{:S(2)}, u32[]{:S(2)}) collective-permute-start(f32[9,8,2,8,128]{4,3,2,1,0:T(8,128)S(1)} %slice.15), channel_id=1, source_target_pairs={{0,4},{4,8},{8,12},{12,16},{16,20},{20,24},{24,28},{28,32},{32,36}... | collective-permute-start | bytes 1769480 | tf_op jit(solution)/shard_map/ppermute | solution.py:401
  72.7 36.7 %all-to-all-start.2 = ((f32[128,4,128]{2,1,0:T(4,128)}), f32[128,4,128]{2,1,0:T(4,128)S(1)}, u32[]{:S(2)}, u32[]{:S(2)}) async-start(f32[128,4,128]{2,1,0:T(4,128)} %get-tuple-element.32), calls=%async_computation.2 | async-start | bytes 524288 | tf_op jit(solution)/shard_map/all_to_all | solution.py:442
  87.5 11.4 %collective-permute-start.4 = (f32[8,5,8,128]{3,2,1,0:T(8,128)S(1)}, f32[8,5,8,128]{3,2,1,0:T(8,128)S(1)}, u32[]{:S(2)}, u32[]{:S(2)}) collective-permute-start(f32[8,5,8,128]{3,2,1,0:T(8,128)S(1)} %get-tuple-element.28), channel_id=1, source_target_pairs={{0,4},{4,8},{8,12},{12,16},{16,20},{20,24},{24,28},{28,32},{32,36}... | collective-permute-start | bytes 491528 | tf_op jit(solution)/shard_map/ppermute | solution.py:401
  90.8 11.0 %collective-permute-start.5 = (f32[8,5,8,128]{3,2,1,0:T(8,128)S(1)}, f32[8,5,8,128]{3,2,1,0:T(8,128)S(1)}, u32[]{:S(2)}, u32[]{:S(2)}) collective-permute-start(f32[8,5,8,128]{3,2,1,0:T(8,128)S(1)} %get-tuple-element.29), channel_id=1, source_target_pairs={{4,0},{8,4},{12,8},{16,12},{20,16},{24,20},{28,24},{32,28},{36,32}... | collective-permute-start | bytes 491528 | tf_op jit(solution)/shard_map/ppermute | solution.py:401

commit v2 on v1

v2 whole, which is shorter than its diff:
```python
import jax
import jax.numpy as jnp
from jax import lax
from jax.experimental import pallas as pl
from jax.experimental.pallas import tpu as pltpu
from jax.sharding import PartitionSpec as P

HOP = 0.12
MU = 0.15
PAIR = 0.3
CAP = 12
LANES = 32
EXACT = lax.Precision.HIGHEST
F32 = jnp.float32
BF16 = jnp.bfloat16


def iota(shape, dim):
    return lax.broadcasted_iota(jnp.int32, shape, dim)


def split(x):
    high = x.astype(BF16)
    return high, (x - high.astype(F32)).astype(BF16)


def dot(a, b):
    return jnp.dot(a, b, preferred_element_type=F32)


def dot3(a, b):
    return dot(a[0], b[0]) + dot(a[0], b[1]) + dot(a[1], b[0])


def dot_rows(a, b):
    return lax.dot_general(a, b, (((1,), (1,)), ((), ())), preferred_element_type=F32)


def beside(s):
    rank = s.ndim
    sub, lane = iota(s.shape, rank - 2), iota(s.shape, rank - 1)
    left = pltpu.roll(s, 1, rank - 1)
    left = jnp.where(lane == 0, pltpu.roll(left, 1, rank - 2), left)
    left = jnp.where((lane == 0) & (sub == 0), 0.0, left)
    right = pltpu.roll(s, 127, rank - 1)
    right = jnp.where(lane == 127, pltpu.roll(right, 7, rank - 2), right)
    right = jnp.where((lane == 127) & (sub == 7), 0.0, right)
    return left + right


def local_part(s, disorder, around):
    inner = (disorder - MU) * s - HOP * around
    return jnp.concatenate(
        [inner[:4] + PAIR * s[4:], PAIR * s[:4] - inner[4:]], axis=0
    )


def signed(s):
    return jnp.concatenate([s[:4], -s[4:]], axis=0)


def stacked(w):
    high, low = split(w)
    return jnp.concatenate([high, low, high], axis=1)


def stacked_right(x):
    high, low = split(x)
    return jnp.concatenate([high, high, low], axis=0)


def route_kernel(
    a_hbm, tile_hbm, spot_hbm, block_hbm, coup_hbm, msg_ref, rank_ref,
    a_ref, tile_ref, spot_ref, block_ref, coup_ref, sems,
):
    pairs = (
        (tile_hbm, tile_ref), (spot_hbm, spot_ref), (a_hbm, a_ref), (block_hbm, block_ref), (coup_hbm, coup_ref)
    )
    copies = [pltpu.make_async_copy(src, dst, sems.at[i]) for i, (src, dst) in enumerate(pairs)]
    for copy in copies:
        copy.start()
    count = a_ref.shape[2]
    tiles = msg_ref.shape[0]
    part = 256
    earlier = (iota((part, part), 0) < iota((part, part), 1)).astype(F32).astype(BF16)
    copies[0].wait()
    hot = (iota((tiles, count), 0) == tile_ref[...]).astype(F32)
    hot16 = hot.astype(BF16)
    ranks, seen = [], jnp.zeros((tiles, 1), F32)
    for k in range(0, count, part):
        chunk = hot[:, k : k + part]
        ranks.append(jnp.sum((dot(hot16[:, k : k + part], earlier) + seen) * chunk, axis=0, keepdims=True))
        seen = seen + jnp.sum(chunk, axis=1, keepdims=True)
    rank = jnp.concatenate(ranks, axis=1).astype(jnp.int32)
    rank_ref[...] = rank
    for copy in copies[1:]:
        copy.wait()
    a = jnp.concatenate([a_ref[:, 0, :], a_ref[:, 1, :]], axis=1)
    c, b = coup_ref[...], block_ref[...]
    cb = jnp.dot(c, b, precision=EXACT, preferred_element_type=F32)
    cbb = jnp.dot(cb, b, precision=EXACT, preferred_element_type=F32)
    pad = jnp.zeros((12, 8), F32)
    w = jnp.concatenate([jnp.concatenate([c, cb, cbb], axis=0), pad], axis=1)
    a = jnp.concatenate([a, jnp.zeros((8, 2 * count), F32)], axis=0)
    g = dot(stacked(w), stacked_right(a))
    val = jnp.concatenate(
        [g[4 * k : 4 * k + 4, v * count : (v + 1) * count] for k in range(3) for v in range(2)], axis=0
    )
    spot = spot_ref[...].reshape(1, count)
    row, col = spot >> 10, spot & 1023
    below = jnp.where(row == 0, col + 1025, 0)
    above = jnp.where(row == 1, col + 1, 0)
    vals = jnp.concatenate(
        [val, (spot + 1).astype(F32), below.astype(F32), above.astype(F32), jnp.zeros((5, count), F32)],
        axis=0,
    )
    slots = split(
        jnp.concatenate([jnp.where(rank == r, vals, 0.0) for r in range(CAP)], axis=0)
    )
    msg = dot_rows(hot16, slots[0]) + dot_rows(hot16, slots[1])
    at, kind = iota(msg.shape, 0), iota(msg.shape, 1) % LANES
    up = jnp.where(at == tiles - 1, 0.0, pltpu.roll(msg, tiles - 1, 0))
    down = jnp.where(at == 0, 0.0, pltpu.roll(msg, 1, 0))
    msg_ref[:, 0, :] = jnp.where(kind == 25, up, jnp.where(kind == 26, down, msg))


CORNER = [(1, 1), (1, 2), (2, 1)]


def pack_kernel(lo_ref, hi_ref, above_ref, below_ref, after_ref, up_ref, down_ref):
    for i, (k, d) in enumerate(CORNER):
        for j, (ref, l) in enumerate(((above_ref, 3 - k), (below_ref, k - 1))):
            up_ref[:, 3 * j + i] = ref[:, l, 2 - d]
            down_ref[:, 3 * j + i] = ref[:, l, d - 1]
    for l in range(4):
        up_ref[:, 6 + l] = lo_ref[:, l, 1]
        down_ref[:, 6 + l] = hi_ref[:, l, 0]


def top_kernel(x_ref, lo_ref, hi_ref, coup_ref, block_ref, top_ref, mix_ref):
    c = coup_ref[...]
    cb = jnp.dot(c, block_ref[...], precision=EXACT, preferred_element_type=F32)
    nt = (((1,), (1,)), ((), ()))
    mix_ref[0] = lax.dot_general(c, c, nt, precision=EXACT, preferred_element_type=F32)
    mix_ref[1] = lax.dot_general(cb, c, nt, precision=EXACT, preferred_element_type=F32)

    def s0(l, r):
        return (lo_ref[:, l, r + 2] if r < 0 else hi_ref[:, l, r - 2] if r > 1 else x_ref[:, l, r])

    for r in range(2):
        rows = pl.ds(8 * r, 8)
        first = []
        for l in range(2):
            here = s0(l, r)
            s = here[:8]
            around = beside(s) + s0(l + 1, r)[:8] + s0(l, r - 1)[:8] + s0(l, r + 1)[:8]
            if l > 0:
                around = around + s0(l - 1, r)[:8]
            first.append(local_part(s, here[8:9], around))
        top_ref[0:8, rows, :] = first[0]
        top_ref[8:16, rows, :] = -2.0 * HOP * signed(first[1]) - s0(0, r)[:8]
        top_ref[16:25, rows, :] = s0(0, r)
        top_ref[25:26, rows, :] = jnp.zeros((1, 8, 128), F32)


def pure_kernel(
    pos_ref, x_ref, lo_ref, hi_ref, low2_ref, high2_ref, above_ref, below_ref, after_ref,
    one_ref, two_ref, s1_ref,
):
    first_layer = pos_ref[0] == 0
    last_layer = pos_ref[0] == pos_ref[1] - 1
    first_row = pos_ref[2] == 0
    last_row = pos_ref[2] == pos_ref[3] - 1

    def masked(s, l, r):
        out = None
        for cond, flag in (
            (l < 0, first_layer), (l > 3, last_layer), (r < 0, first_row), (r > 1, last_row)
        ):
            if cond:
                out = flag if out is None else out | flag
        return s if out is None else jnp.where(out, 0.0, s)

    def start(l, r):
        k, d = max(-l, l - 3), max(-r, r - 1)
        side = low2_ref if r < 0 else high2_ref
        if k > 0 and d > 0:
            return side[:, (0 if l < 0 else 3) + CORNER.index((k, d))]
        if k > 0:
            return above_ref[:, 3 - k, r] if l < 0 else below_ref[:, k - 1, r]
        if d > 2:
            return side[:, 6 + l]
        return (lo_ref[:, l, r + 2] if r < 0 else hi_ref[:, l, r - 2] if r > 1 else x_ref[:, l, r])

    def s0(l, r):
        return start(l, r)[:8]

    def beyond(l, r):
        return max(-l, l - 3, 0) + max(-r, r - 1, 0)

    for l in range(-2, 6):
        for r in range(-2, 4):
            if beyond(l, r) > 2:
                continue
            here = start(l, r)
            s = here[:8]
            around = beside(s) + s0(l - 1, r) + s0(l + 1, r) + s0(l, r - 1) + s0(l, r + 1)
            s1_ref[:, l + 2, r + 2] = masked(local_part(s, here[8:9], around), l, r)
    for l in range(-1, 5):
        for r in range(-1, 3):
            if beyond(l, r) > 1:
                continue
            s = s1_ref[:, l + 2, r + 2]
            around = beside(s) + s1_ref[:, l + 1, r + 2] + s1_ref[:, l + 3, r + 2]
            around = around + s1_ref[:, l + 2, r + 1] + s1_ref[:, l + 2, r + 3]
            new = 2.0 * local_part(s, start(l, r)[8:9], around) - s0(l, r)
            two_ref[:, l + 1, r + 1] = masked(new, l, r)
            if beyond(l, r) == 0:
                one_ref[:, l, r] = s


def columns(got):
    width = got.shape[1] // 128
    return jnp.concatenate([got[:, 128 * j : 128 * (j + 1)].T for j in range(width)], axis=0)


def scatter_kernel(pos_ref, got_ref, top_ref, out_ref, d2_ref, site_ref, dense_ref):
    got = got_ref[:, 0, :]
    tiles = got.shape[0]
    slots = columns(got)
    sub = iota((256, tiles), 0)
    total = None
    for r in range(CAP):
        vals = slots[r * LANES : r * LANES + 24]
        sites = slots[r * LANES + 24 : r * LANES + 27].astype(jnp.int32) - 1
        site_ref[r : r + 1] = sites[0:1]
        site_ref[16 + r : 17 + r] = sites[1:2]
        site_ref[32 + r : 33 + r] = sites[2:3]
        high = sites[0:1] >> 8
        near = vals.astype(BF16).astype(F32)
        number = (iota((8, tiles), 0) == high).astype(F32)
        left = jnp.concatenate(
            [
                jnp.concatenate([jnp.where(high == h, part, 0.0) for h in range(8)] + [last], axis=0)
                for part, last in ((near, number), (vals - near, jnp.zeros_like(number)))
            ],
            axis=1,
        ).astype(BF16)
        right = (sub == (sites[0:1] & 255)).astype(F32).astype(BF16)
        part = dot_rows(left, jnp.concatenate([right, right], axis=1))
        total = part if total is None else total + part
    dense_ref[0] = total[:, :128]
    dense_ref[1] = total[:, 128:]

    on = pos_ref[0] == 0
    for j in range(2):
        rows = pl.ds(j, 8, stride=2)

        def dense(k):
            k = k - k % 8 + (k % 2) * 4 + (k % 8) // 2
            return dense_ref[j, pl.ds(k, 8, stride=24), :]

        for k in range(8):
            q1 = dense(k) + jnp.where(on, top_ref[k, rows, :], 0.0)
            q2 = 2.0 * dense(8 + k) + jnp.where(on, top_ref[8 + k, rows, :], 0.0)
            d2 = dense(16 + k)
            d2_ref[k, rows, :] = d2
            tail = jnp.where(on, top_ref[16 + k, rows, :], d2)
            for y in range(4):
                out_ref[y, k, rows, :] = q1
                out_ref[y, 8 + k, rows, :] = q2
                out_ref[y, 16 + k, rows, :] = tail
        field = jnp.where(on, top_ref[24, rows, :], 0.0)
        for y in range(4):
            out_ref[y, 24, rows, :] = field
            out_ref[y, 25, rows, :] = dense_ref[j, 192:200, :]


def evolve_kernel(
    pos_ref, m_ref, top_ref, d2_ref, site_ref, mix_ref,
    ans_ref, d_ref, f_ref, f1_ref,
):
    tiles = site_ref.shape[1]
    on = pos_ref[0] == 0
    kk, kb = mix_ref[0], mix_ref[1]

    def mix(k, s):
        def row(o):
            terms = [k[o : o + 1, q : q + 1] * s[2 * q : 2 * q + 2] for q in range(4)]
            return (terms[0] + terms[1]) + (terms[2] + terms[3])

        return jnp.concatenate([row(o) for o in range(4)], axis=0)

    def rows_of(s):
        return s.reshape(s.shape[0], 2, 8, 128)

    s0 = m_ref[0, 16:24]
    field = rows_of(m_ref[0, 24:25])
    s1 = (m_ref[0, 0:8] + m_ref[1, 0:8]) + (m_ref[2, 0:8] + m_ref[3, 0:8])
    q2 = (m_ref[0, 8:16] + m_ref[1, 8:16]) + (m_ref[2, 8:16] + m_ref[3, 8:16])
    number = (m_ref[0, 25:26] + m_ref[1, 25:26]) + (m_ref[2, 25:26] + m_ref[3, 25:26])

    def flat_part(s):
        s = rows_of(s)
        other = jnp.concatenate([s[:, 1:2], s[:, 0:1]], axis=1)
        return local_part(s, field, beside(s) + other).reshape(8, 16, 128)

    hopped = q2 + 2.0 * (number * mix(kk, s0))
    s2 = hopped + 2.0 * flat_part(s1)
    d0 = jnp.where(on, s1 - top_ref[0:8], 0.0)
    delta = jnp.where(on, hopped - top_ref[8:16] + 2.0 * flat_part(d0), 0.0)
    d2 = d2_ref[...] + (m_ref[1, 16:24] + m_ref[2, 16:24] + m_ref[3, 16:24])
    third = 2.0 * (d2 + number * (mix(kb, s0) + mix(kk, s1))) - d0
    d_ref[0:8] = d0
    d_ref[8:16] = delta
    d_ref[16:24] = jnp.where(on, third, 0.0)
    for k in range(8):
        f_ref[pl.ds(k, 16, stride=24), :] = s0[k]
        f_ref[pl.ds(8 + k, 16, stride=24), :] = s1[k]
        f_ref[pl.ds(16 + k, 16, stride=24), :] = s2[k]
        f1_ref[pl.ds(k, 16, stride=8), :] = s1[k]
    f = jnp.concatenate(split(f_ref[...]), axis=1)
    f1 = jnp.concatenate(split(f1_ref[...]), axis=1)
    sub = iota((128, 2 * tiles), 0)

    def pick(table, width, sites):
        right = (sub == (sites & 127)).astype(F32).astype(BF16)
        found = dot(table, jnp.concatenate([right, right], axis=0))
        high = sites >> 7
        out = jnp.zeros((width, sites.shape[1]), F32)
        for h in range(16):
            out = out + jnp.where(high == h, found[h * width : (h + 1) * width], 0.0)
        return out

    own, low, high = [], [], []
    for r in range(0, CAP, 2):
        for table, width, base, out in ((f, 24, 0, own), (f1, 8, 16, low), (f1, 8, 32, high)):
            sites = jnp.concatenate(
                [site_ref[base + r : base + r + 1], site_ref[base + r + 1 : base + r + 2]], axis=1
            )
            both = pick(table, width, sites)
            out += [both[:, :tiles], both[:, tiles:]]
    answer = jnp.concatenate(own + low + high + [jnp.zeros((32, tiles), F32)], axis=0)
    for j in range(4):
        ans_ref[:, j, :] = answer[128 * j : 128 * (j + 1)].T


def adatom_kernel(a_ref, back_ref, tile_ref, rank_ref, block_ref, coup_ref, prev_ref, last_ref):
    count = a_ref.shape[2]
    tiles = back_ref.shape[0]
    back = jnp.concatenate([back_ref[:, j, :].T for j in range(4)], axis=0)
    back = jnp.concatenate(
        [back[:288], pltpu.roll(back[288:384], 1, 1), pltpu.roll(back[384:480], tiles - 1, 1)], axis=0
    )
    hot = (iota((tiles, count), 0) == tile_ref[...]).astype(F32).astype(BF16)
    found = dot(jnp.concatenate(split(back), axis=1), jnp.concatenate([hot, hot], axis=0))
    rank = rank_ref[...]
    s = jnp.zeros((24, count), F32)
    halo = jnp.zeros((8, count), F32)
    for r in range(CAP):
        here = rank == r
        s = s + jnp.where(here, found[24 * r : 24 * r + 24], 0.0)
        near = found[288 + 8 * r : 296 + 8 * r] + found[384 + 8 * r : 392 + 8 * r]
        halo = halo + jnp.where(here, near, 0.0)
    sign = jnp.where(iota((8, count), 0) < 4, 1.0, -1.0)
    s2 = s[16:24] - 2.0 * HOP * sign * halo
    i, j = iota((4, 8), 0), iota((4, 8), 1)
    spread = (i == j // 2).astype(F32)
    c = lax.dot_general(
        coup_ref[...], spread, (((0,), (0,)), ((), ())), precision=EXACT, preferred_element_type=F32
    )
    w = stacked(jnp.concatenate([block_ref[...], c], axis=1))
    even = iota((8, count), 0) % 2 == 0

    def apply(a, s):
        s = jnp.concatenate([jnp.where(even, s, 0.0), jnp.where(even, 0.0, s)], axis=1)
        return dot(w, stacked_right(jnp.concatenate([a, s], axis=0)))

    a0 = jnp.concatenate([a_ref[:, 0, :], a_ref[:, 1, :]], axis=1)
    a1 = apply(a0, s[0:8])
    a2 = 2.0 * apply(a1, s[8:16]) - a0
    a3 = 2.0 * apply(a2, s2) - a1
    for v in range(2):
        prev_ref[:, v, :] = a2[:, v * count : (v + 1) * count]
        last_ref[:, v, :] = a3[:, v * count : (v + 1) * count]


def last_kernel(pos_ref, x_ref, one_ref, two_ref, d_ref, before_ref, after_ref, prev_ref, last_ref):
    has_before = pos_ref[2] > 0
    has_after = pos_ref[2] < pos_ref[3] - 1
    d0 = d_ref[0:8].reshape(8, 2, 8, 128)
    delta = d_ref[8:16].reshape(8, 2, 8, 128)
    third = d_ref[16:24].reshape(8, 2, 8, 128)

    def hop(s):
        return -2.0 * HOP * signed(s)

    hop0 = [hop(d0[:, r]) for r in range(2)]
    for r, ref in ((0, before_ref), (1, after_ref)):
        prev_ref[:, 0, r] = two_ref[:, 1, r + 1] + delta[:, r] + hop(ref[0:8])
        prev_ref[:, 1, r] = two_ref[:, 2, r + 1] + hop0[r]
        prev_ref[:, 2, r] = two_ref[:, 3, r + 1]
        prev_ref[:, 3, r] = two_ref[:, 4, r + 1]

    def beyond(l, r):
        ref, there = (before_ref, has_before) if r == 0 else (after_ref, has_after)
        s = two_ref[:, l + 1, 3 * r]
        if l == 0:
            s = s + ref[8:16] + jnp.where(there, hop0[r], 0.0)
        if l == 1:
            s = s + hop(ref[0:8])
        return s

    for l in range(4):
        for r in range(2):
            s = prev_ref[:, l, r]
            over = two_ref[:, 0, r + 1] if l == 0 else prev_ref[:, l - 1, r]
            under = two_ref[:, 5, r + 1] if l == 3 else prev_ref[:, l + 1, r]
            around = beside(s) + over + under + prev_ref[:, l, 1 - r] + beyond(l, r)
            new = 2.0 * local_part(s, x_ref[8:9, l, r], around) - one_ref[:, l, r]
            if l == 0:
                new = new + 2.0 * third[:, r] - d0[:, r]
            last_ref[:, l, r] = new


VM = pl.BlockSpec(memory_space=pltpu.VMEM)
SM = pl.BlockSpec(memory_space=pltpu.SMEM)


def shape(*dims, dtype=F32):
    return jax.ShapeDtypeStruct(dims, dtype)


def call(kernel, name, outs, args, scratch=(), smem=False, cost=0, space=pltpu.VMEM, limit=16):
    return pl.pallas_call(
        kernel,
        out_shape=outs,
        in_specs=[SM if smem and i == 0 else pl.BlockSpec(memory_space=space) for i in range(len(args))],
        out_specs=[VM] * len(outs),
        scratch_shapes=list(scratch),
        name=name,
        cost_estimate=pl.CostEstimate(flops=cost, bytes_accessed=0, transcendentals=0),
        compiler_params=pltpu.CompilerParams(vmem_limit_bytes=limit * 2**20),
    )(*args)


def per_device(
    substrate_start, adatom_start, disorder, adatom_block, coupling, adatom_tile, adatom_spot
):
    tiles, depths = lax.axis_size("tile"), lax.axis_size("depth")
    t, y = lax.axis_index("tile"), lax.axis_index("depth")
    count = adatom_spot.shape[0]
    pos = jnp.stack([y, jnp.int32(depths), t, jnp.int32(tiles)])

    def shifted(x, axis, size, step):
        pairs = [(i, i + step) for i in range(size) if 0 <= i + step < size]
        return lax.ppermute(x, axis, pairs)

    own_tile = adatom_tile.reshape(1, count)
    msg, rank = call(
        route_kernel, "route",
        (shape(tiles, 1, CAP * LANES), shape(1, count, dtype=jnp.int32)),
        (adatom_start, own_tile, adatom_spot, adatom_block, coupling),
        (
            pltpu.VMEM((40, 2, count), F32), pltpu.VMEM((1, count), jnp.int32), pltpu.VMEM((count,), jnp.int32),
            pltpu.VMEM((40, 40), F32), pltpu.VMEM((4, 40), F32), pltpu.SemaphoreType.DMA((5,)),
        ),
        space=pl.ANY, limit=60
    )
    substrate, disorder, rank = lax.optimization_barrier((substrate_start, disorder, rank))
    got = lax.all_to_all(msg, "tile", split_axis=0, concat_axis=0, tiled=True)
    x = jnp.concatenate(
        [substrate.reshape(8, 4, 2, 8, 128), disorder.reshape(1, 4, 2, 8, 128)], axis=0
    )
    lo = shifted(x, "tile", tiles, 1)
    hi = shifted(x, "tile", tiles, -1)
    above = shifted(x[:, 1:], "depth", depths, 1)
    below = shifted(x[:, :3], "depth", depths, -1)
    top, mix = call(
        top_kernel, "top", (shape(26, 16, 128), shape(2, 4, 4)), (x, lo, hi, coupling, adatom_block)
    )
    part, d2, site = call(
        scatter_kernel, "scatter",
        (shape(4, 26, 16, 128), shape(8, 16, 128), shape(48, tiles, dtype=jnp.int32)),
        (pos, got, top),
        (pltpu.VMEM((2, 200, 128), F32),), smem=True,
    )
    above, below, part = lax.optimization_barrier((above, below, part))
    up, down = call(
        pack_kernel, "pack", (shape(9, 10, 8, 128), shape(9, 10, 8, 128)), (lo, hi, above, below, site)
    )
    low2 = shifted(up, "tile", tiles, 1)
    high2 = shifted(down, "tile", tiles, -1)
    part = lax.all_to_all(part, "depth", split_axis=0, concat_axis=0, tiled=True)
    answer, d = call(
        evolve_kernel, "evolve",
        (shape(tiles, 4, 128), shape(24, 16, 128)),
        (pos, part, top, d2, site, mix),
        (pltpu.VMEM((384, 128), F32), pltpu.VMEM((128, 128), F32)), smem=True,
    )
    before = shifted(d[:16, 8:], "tile", tiles, 1)
    after = shifted(d[:16, :8], "tile", tiles, -1)
    one, two = call(
        pure_kernel, "pure",
        (shape(8, 4, 2, 8, 128), shape(8, 6, 4, 8, 128)),
        (pos, x, lo, hi, low2, high2, above, below, d),
        (pltpu.VMEM((8, 8, 6, 8, 128), F32),), smem=True, cost=10**10,
    )
    back = lax.all_to_all(answer, "tile", split_axis=0, concat_axis=0, tiled=True)
    sub_prev, sub_last = call(
        last_kernel, "last",
        (shape(8, 4, 2, 8, 128), shape(8, 4, 2, 8, 128)),
        (pos, x, one, two, d, before, after), smem=True,
    )
    ad_prev, ad_last = call(
        adatom_kernel, "adatoms",
        (shape(40, 2, count), shape(40, 2, count)),
        (adatom_start, back, own_tile, rank, adatom_block, coupling),
    )
    return (
        sub_prev.reshape(4, 2, 4, 2, 1024),
        sub_last.reshape(4, 2, 4, 2, 1024),
        ad_prev,
        ad_last,
    )


def solution(mesh):
    in_specs = (
        P(None, None, "depth", "tile", None),
        P(None, None, ("tile", "depth")),
        P("depth", "tile", None),
        P(),
        P(),
        P(("tile", "depth"), None),
        P(("tile", "depth")),
    )
    out_specs = (
        P(None, None, "depth", "tile", None),
        P(None, None, "depth", "tile", None),
        P(None, None, ("tile", "depth")),
        P(None, None, ("tile", "depth")),
    )
    return jax.shard_map(
        per_device, mesh=mesh, in_specs=in_specs, out_specs=out_specs, check_vma=False
    )
```

time: 114 us -> 102 us (0.89)
  blocking collectives: 17.5 us -> 0 us
  starting transfers between devices: 52.3 us -> 58.2 us
  local copies, waits for them, and re-layouts: 6.07 us -> 2.54 us
  waiting for transfers between devices: 23.8 us -> 25.4 us
  Pallas kernels: 12.4 us -> 13.7 us
    all_to_all x1 -> x0, blocking collectives: 17.5 us -> none  [per_device(): lax.all_to_all(part, 'depth', split_axis=0, concat_axis=0, tiled=True)]
    ppermute x6 -> x8, waiting for transfers between devices: 17.8 us -> 9.72 us  [shifted(): return lax.ppermute(x, axis, pairs)]
    all_to_all x0 -> x1, waiting for transfers between devices: none -> 5.27 us  [per_device(): lax.all_to_all(part, 'depth', split_axis=0, concat_axis=0, tiled=True)]
    all_to_all x0 -> x1, starting transfers between devices: none -> 4.19 us  [per_device(): lax.all_to_all(part, 'depth', split_axis=0, concat_axis=0, tiled=True)]
    ppermute x6 -> x8, starting transfers between devices: 17.6 us -> 21.4 us  [shifted(): return lax.ppermute(x, axis, pairs)]
    all_to_all x1, waiting for transfers between devices: 0.95 us -> 3.66 us  [per_device(): got = lax.all_to_all(msg, 'tile', split_axis=0, concat_axis=0, tiled=True)]
    all_to_all x1, starting transfers between devices: 14.8 us -> 12.8 us  [per_device(): lax.all_to_all(answer, 'tile', split_axis=0, concat_axis=0, tiled=True)]
    unnamed x14 -> x15, local copies, waits for them, and re-layouts: 2.37 us -> 0.58 us
  transfers between devices with their start and end apart: 8 -> 11, of which waited for: 5 -> 6; matrix products, arithmetic and copies ran while one was open for 2% -> 2% of each run, Pallas kernels for 4% -> 9%
where the time goes in v2:
time: 102 us; the launch traced here: 101 us
  starting transfers between devices  58.2 us (57%)
  waiting for transfers between devices  25.4 us (25%)
  Pallas kernels  13.7 us (13%)
  local copies, waits for them, and re-layouts  2.54 us (2%)
    ppermute x8, starting transfers between devices, shifted(): return lax.ppermute(x, axis, pairs)  21.4 us
    all_to_all x1, starting transfers between devices, per_device(): got = lax.all_to_all(msg, 'tile', split_axis=0, concat_axis=0, tiled=True)  19.8 us
    pallas_call x8, Pallas kernels, call(): pl.pallas_call(kernel, out_shape=outs, in_specs=[SM if smem and i == 0 el...  13.7 us
    all_to_all x1, starting transfers between devices, per_device(): lax.all_to_all(answer, 'tile', split_axis=0, concat_axis=0, tiled=True)  12.8 us
    ppermute x8, waiting for transfers between devices, shifted(): return lax.ppermute(x, axis, pairs)  9.72 us
    all_to_all x1, waiting for transfers between devices, per_device(): lax.all_to_all(answer, 'tile', split_axis=0, concat_axis=0, tiled=True)  6.77 us
    all_to_all x1, waiting for transfers between devices, per_device(): lax.all_to_all(part, 'depth', split_axis=0, concat_axis=0, tiled=True)  5.27 us
    all_to_all x1, starting transfers between devices, per_device(): lax.all_to_all(part, 'depth', split_axis=0, concat_axis=0, tiled=True)  4.19 us
  transfers between devices with their start and end apart: 11, of which 6 were waited for; matrix products, arithmetic and copies ran while one was open for 2% of the time, Pallas kernels for 9%

profile of v2, /device:TPU:7, one launch (start us, length us, event | category | flops | bytes accessed | tf_op | source)
XLA Modules:
  0.0 100.8 jit_solution(2950008575273268399)
XLA Ops:
  0.6 2.8 %route.1 = (f32[128,1,384]{2,1,0:T(1,128)}, s32[1,768]{1,0:T(1,128)}) custom-call(f32[40,2,768]{2,1,0:T(2,128)} %a_ref.1, s32[1,768]{1,0:T(1,128)} %bitcast.7, s32[768]{0:T(1024)} %spot_hbm.1, f32[40,40]{1,0:T(8,128)} %block_ref.3, f32[4,40]{1,0:T(4,128)} %coup_ref.3), custom_call_target="tpu_custom_call" | custom-call | tf_op jit(solution)/shard_map/route/pallas_call | solution.py:435
  3.5 0.0 copy-start.5
  3.5 19.8 %all-to-all-start = ((f32[128,1,384]{2,1,0:T(1,128)}), f32[128,1,384]{2,1,0:T(1,128)S(1)}, u32[]{:S(2)}, u32[]{:S(2)}) async-start(f32[128,1,384]{2,1,0:T(1,128)} %get-tuple-element.30), calls=%async_computation | async-start | bytes 393216 | tf_op jit(solution)/shard_map/all_to_all | solution.py:471
  23.3 0.0 copy-done.5
  23.3 0.0 copy-start.6
  23.3 0.2 reshape.24
  23.5 0.5 copy-done.6
  24.1 3.3 %collective-permute-start = (f32[9,4,2,8,128]{4,3,2,1,0:T(8,128)S(1)}, f32[9,4,2,8,128]{4,3,2,1,0:T(8,128)S(1)}, u32[]{:S(2)}, u32[]{:S(2)}) collective-permute-start(f32[9,4,2,8,128]{4,3,2,1,0:T(8,128)S(1)} %constant_dynamic-update-slice_fusion.x_ref), channel_id=1, source_target_pairs={{0,4},{4,8},{8,12},{12,16},{16,20},{20,24},{24,28},{28,32},{32,36}... | collective-permute-start | bytes 884744 | tf_op jit(solution)/shard_map/ppermute | solution.py:457
  27.5 1.9 %collective-permute-start.1 = (f32[9,4,2,8,128]{4,3,2,1,0:T(8,128)S(1)}, f32[9,4,2,8,128]{4,3,2,1,0:T(8,128)S(1)}, u32[]{:S(2)}, u32[]{:S(2)}) collective-permute-start(f32[9,4,2,8,128]{4,3,2,1,0:T(8,128)S(1)} %constant_dynamic-update-slice_fusion.x_ref), channel_id=1, source_target_pairs={{4,0},{8,4},{12,8},{16,12},{20,16},{24,20},{28,24},{32,28},{36,32}... | collective-permute-start | bytes 884744 | tf_op jit(solution)/shard_map/ppermute | solution.py:457
  29.4 0.0 copy-start.2
  29.5 0.0 copy-start.1
  29.5 3.2 %collective-permute-start.2 = (f32[9,3,2,8,128]{4,3,2,1,0:T(8,128)S(1)}, f32[9,3,2,8,128]{4,3,2,1,0:T(8,128)S(1)}, u32[]{:S(2)}, u32[]{:S(2)}) collective-permute-start(f32[9,3,2,8,128]{4,3,2,1,0:T(8,128)S(1)} %get-tuple-element.51), channel_id=1, source_target_pairs={{0,1},{1,2},{2,3},{4,5},{5,6},{6,7},{8,9},{9,10},{10,11},{12,13},{... | collective-permute-start | bytes 663560 | tf_op jit(solution)/shard_map/ppermute | solution.py:457
  32.7 1.3 %collective-permute-start.3 = (f32[9,3,2,8,128]{4,3,2,1,0:T(8,128)S(1)}, f32[9,3,2,8,128]{4,3,2,1,0:T(8,128)S(1)}, u32[]{:S(2)}, u32[]{:S(2)}) collective-permute-start(f32[9,3,2,8,128]{4,3,2,1,0:T(8,128)S(1)} %get-tuple-element.50), channel_id=1, source_target_pairs={{1,0},{2,1},{3,2},{5,4},{6,5},{7,6},{9,8},{10,9},{11,10},{13,12},{... | collective-permute-start | bytes 663560 | tf_op jit(solution)/shard_map/ppermute | solution.py:457
  34.0 0.1 pad_add_fusion.pos_ref
  34.1 1.4 %collective-permute-done.lo_ref = f32[9,4,2,8,128]{4,3,2,1,0:T(8,128)S(1)} collective-permute-done((f32[9,4,2,8,128]{4,3,2,1,0:T(8,128)S(1)}, f32[9,4,2,8,128]{4,3,2,1,0:T(8,128)S(1)}, u32[]{:S(2)}, u32[]{:S(2)}) %collective-permute-start) | collective-permute-done | bytes 294944 | tf_op jit(solution)/shard_map/ppermute | solution.py:457
  35.5 2.9 %collective-permute-done.1.hi_ref = f32[9,4,2,8,128]{4,3,2,1,0:T(8,128)S(1)} collective-permute-done((f32[9,4,2,8,128]{4,3,2,1,0:T(8,128)S(1)}, f32[9,4,2,8,128]{4,3,2,1,0:T(8,128)S(1)}, u32[]{:S(2)}, u32[]{:S(2)}) %collective-permute-start.1) | collective-permute-done | bytes 294944 | tf_op jit(solution)/shard_map/ppermute | solution.py:457
  38.3 0.0 copy-done.2
  38.3 0.0 copy-done.1
  38.3 0.3 top.1
  38.6 3.7 %all-to-all-done.got_ref = f32[128,1,384]{2,1,0:T(1,128)S(1)} async-done(((f32[128,1,384]{2,1,0:T(1,128)}), f32[128,1,384]{2,1,0:T(1,128)S(1)}, u32[]{:S(2)}, u32[]{:S(2)}) %all-to-all-start) | async-done | bytes 196640 | tf_op jit(solution)/shard_map/all_to_all | solution.py:471
  42.3 2.3 %scatter.1 = (f32[4,26,16,128]{3,2,1,0:T(8,128)}, f32[8,16,128]{2,1,0:T(8,128)S(1)}, s32[48,128]{1,0:T(8,128)S(1)}) custom-call(s32[4]{0:T(128)S(1)} %pad_add_fusion.pos_ref, f32[128,1,384]{2,1,0:T(1,128)S(1)} %all-to-all-done.got_ref, f32[26,16,128]{2,1,0:T(8,128)S(1)} %get-tuple-element.31.top_ref), custom_call_target="tpu_custom_call" | custom-call | tf_op jit(solution)/shard_map/scatter/pallas_call | solution.py:435
  44.6 0.0 collective-permute-done.2.above_ref
  44.6 0.0 collective-permute-done.3.below_ref
  44.6 4.2 %all-to-all-start.1 = ((f32[4,26,16,128]{3,2,1,0:T(8,128)}), f32[4,26,16,128]{3,2,1,0:T(8,128)S(1)}, u32[]{:S(2)}, u32[]{:S(2)}) async-start(f32[4,26,16,128]{3,2,1,0:T(8,128)} %get-tuple-element.38), calls=%async_computation.1 | async-start | bytes 1703936 | tf_op jit(solution)/shard_map/all_to_all | solution.py:494
  48.8 1.0 pack.1
  49.8 4.4 %collective-permute-start.4 = (f32[9,10,8,128]{3,2,1,0:T(8,128)}, f32[9,10,8,128]{3,2,1,0:T(8,128)S(1)}, u32[]{:S(2)}, u32[]{:S(2)}) collective-permute-start(f32[9,10,8,128]{3,2,1,0:T(8,128)} %get-tuple-element.36), channel_id=1, source_target_pairs={{0,4},{4,8},{8,12},{12,16},{16,20},{20,24},{24,28},{28,32},{32,36}... | collective-permute-start | bytes 1105928 | tf_op jit(solution)/shard_map/ppermute | solution.py:457
  54.2 1.9 %collective-permute-start.5 = (f32[9,10,8,128]{3,2,1,0:T(8,128)}, f32[9,10,8,128]{3,2,1,0:T(8,128)S(1)}, u32[]{:S(2)}, u32[]{:S(2)}) collective-permute-start(f32[9,10,8,128]{3,2,1,0:T(8,128)} %get-tuple-element.37), channel_id=1, source_target_pairs={{4,0},{8,4},{12,8},{16,12},{20,16},{24,20},{28,24},{32,28},{36,32}... | collective-permute-start | bytes 1105928 | tf_op jit(solution)/shard_map/ppermute | solution.py:457
  56.1 5.3 %all-to-all-done.1.m_ref = f32[4,26,16,128]{3,2,1,0:T(8,128)S(1)} async-done(((f32[4,26,16,128]{3,2,1,0:T(8,128)}), f32[4,26,16,128]{3,2,1,0:T(8,128)S(1)}, u32[]{:S(2)}, u32[]{:S(2)}) %all-to-all-start.1) | async-done | bytes 852000 | tf_op jit(solution)/shard_map/all_to_all | solution.py:494
  61.4 2.6 %evolve.1 = (f32[128,4,128]{2,1,0:T(4,128)}, f32[24,16,128]{2,1,0:T(8,128)S(1)}) custom-call(s32[4]{0:T(128)S(1)} %pad_add_fusion.pos_ref, f32[4,26,16,128]{3,2,1,0:T(8,128)S(1)} %all-to-all-done.1.m_ref, f32[26,16,128]{2,1,0:T(8,128)S(1)} %get-tuple-element.31.top_ref, f32[8,16,128]{2,1,0:T(8,128)S(1)} %get-tuple-element.39.d2_ref, ...), custom_call_target="tpu_custom_call" | custom-call | tf_op jit(solution)/shard_map/evolve/pallas_call | solution.py:435
  64.0 12.8 %all-to-all-start.2 = ((f32[128,4,128]{2,1,0:T(4,128)}), f32[128,4,128]{2,1,0:T(4,128)S(1)}, u32[]{:S(2)}, u32[]{:S(2)}) async-start(f32[128,4,128]{2,1,0:T(4,128)} %get-tuple-element.46), calls=%async_computation.2 | async-start | bytes 524288 | tf_op jit(solution)/shard_map/all_to_all | solution.py:509
  76.9 3.3 %collective-permute-start.6 = (f32[16,8,128]{2,1,0:T(8,128)S(1)}, f32[16,8,128]{2,1,0:T(8,128)S(1)}, u32[]{:S(2)}, u32[]{:S(2)}) collective-permute-start(f32[16,8,128]{2,1,0:T(8,128)S(1)} %get-tuple-element.53), channel_id=1, source_target_pairs={{0,4},{4,8},{8,12},{12,16},{16,20},{20,24},{24,28},{28,32},{32,36}... | collective-permute-start | bytes 196616 | tf_op jit(solution)/shard_map/ppermute | solution.py:457
  80.2 1.9 %collective-permute-start.7 = (f32[16,8,128]{2,1,0:T(8,128)S(1)}, f32[16,8,128]{2,1,0:T(8,128)S(1)}, u32[]{:S(2)}, u32[]{:S(2)}) collective-permute-start(f32[16,8,128]{2,1,0:T(8,128)S(1)} %get-tuple-element.52), channel_id=1, source_target_pairs={{4,0},{8,4},{12,8},{16,12},{20,16},{24,20},{28,24},{32,28},{36,32}... | collective-permute-start | bytes 196616 | tf_op jit(solution)/shard_map/ppermute | solution.py:457
  82.2 0.0 collective-permute-done.4.low2_ref
  82.2 0.0 collective-permute-done.5.high2_ref
  82.2 1.8 %pure.1 = (f32[8,4,2,8,128]{4,3,2,1,0:T(8,128)S(1)}, f32[8,6,4,8,128]{4,3,2,1,0:T(8,128)S(1)}) custom-call(s32[4]{0:T(128)S(1)} %pad_add_fusion.pos_ref, f32[9,4,2,8,128]{4,3,2,1,0:T(8,128)S(1)} %constant_dynamic-update-slice_fusion.x_ref, f32[9,4,2,8,128]{4,3,2,1,0:T(8,128)S(1)} %collective-permute-done.lo_ref, ...), custom_call_target="tpu_custom_call" | custom-call | flops 10000000000 | tf_op jit(solution)/shard_map/pure/pallas_call | solution.py:435
  84.0 0.0 collective-permute-done.6.before_ref
  84.0 5.5 %collective-permute-done.7.after_ref = f32[16,8,128]{2,1,0:T(8,128)S(1)} collective-permute-done((f32[16,8,128]{2,1,0:T(8,128)S(1)}, f32[16,8,128]{2,1,0:T(8,128)S(1)}, u32[]{:S(2)}, u32[]{:S(2)}) %collective-permute-start.7) | collective-permute-done | bytes 65568 | tf_op jit(solution)/shard_map/ppermute | solution.py:457
  89.5 0.8 last.1
  90.3 0.8 reshape.26
  91.1 0.0 copy-start
  91.1 0.0 copy-start.3
  91.1 0.0 copy-start.4
  91.1 0.8 reshape.27
  92.0 6.8 %all-to-all-done.2.back_ref = f32[128,4,128]{2,1,0:T(4,128)S(1)} async-done(((f32[128,4,128]{2,1,0:T(4,128)}), f32[128,4,128]{2,1,0:T(4,128)S(1)}, u32[]{:S(2)}, u32[]{:S(2)}) %all-to-all-start.2) | async-done | bytes 262176 | tf_op jit(solution)/shard_map/all_to_all | solution.py:509
  98.7 0.0 copy-done
  98.7 0.0 copy-done.3
  98.7 0.0 copy-done.4
  98.7 2.0 %adatoms.1 = (f32[40,2,768]{2,1,0:T(2,128)}, f32[40,2,768]{2,1,0:T(2,128)}) custom-call(f32[40,2,768]{2,1,0:T(2,128)S(1)} %copy-done, f32[128,4,128]{2,1,0:T(4,128)S(1)} %all-to-all-done.2.back_ref, s32[1,768]{1,0:T(1,128)S(1)} %bitcast.8, s32[1,768]{1,0:T(1,128)S(1)} %copy-done.4, f32[40,40]{1,0:T(8,128)S(1)} %copy-done.1, f32[4,40]{1,0:T(4,128)S(1)} %copy-done.2), custom_call_target="tpu_custom_call" | custom-call | tf_op jit(solution)/shard_map/adatoms/pallas_call | solution.py:435
  (5 shorter events, 0.1 us)
Async XLA Ops:
  3.5 19.8 %copy-start.5 = (f32[4,2,4,2,1024]{4,3,2,1,0:T(2,128)S(1)}, f32[4,2,4,2,1024]{4,3,2,1,0:T(2,128)}, u32[]{:S(2)}) copy-start(f32[4,2,4,2,1024]{4,3,2,1,0:T(2,128)} %param.7) | copy-start | bytes 786436
  3.5 38.8 %all-to-all-start = ((f32[128,1,384]{2,1,0:T(1,128)}), f32[128,1,384]{2,1,0:T(1,128)S(1)}, u32[]{:S(2)}, u32[]{:S(2)}) async-start(f32[128,1,384]{2,1,0:T(1,128)} %get-tuple-element.30), calls=%async_computation | async-start | bytes 393216 | tf_op jit(solution)/shard_map/all_to_all | solution.py:471
  23.3 0.8 copy-start.6
  24.1 11.3 %collective-permute-start = (f32[9,4,2,8,128]{4,3,2,1,0:T(8,128)S(1)}, f32[9,4,2,8,128]{4,3,2,1,0:T(8,128)S(1)}, u32[]{:S(2)}, u32[]{:S(2)}) collective-permute-start(f32[9,4,2,8,128]{4,3,2,1,0:T(8,128)S(1)} %constant_dynamic-update-slice_fusion.x_ref), channel_id=1, source_target_pairs={{0,4},{4,8},{8,12},{12,16},{16,20},{20,24},{24,28},{28,32},{32,36}... | collective-permute-start | bytes 884744 | tf_op jit(solution)/shard_map/ppermute | solution.py:457
  27.5 10.8 %collective-permute-start.1 = (f32[9,4,2,8,128]{4,3,2,1,0:T(8,128)S(1)}, f32[9,4,2,8,128]{4,3,2,1,0:T(8,128)S(1)}, u32[]{:S(2)}, u32[]{:S(2)}) collective-permute-start(f32[9,4,2,8,128]{4,3,2,1,0:T(8,128)S(1)} %constant_dynamic-update-slice_fusion.x_ref), channel_id=1, source_target_pairs={{4,0},{8,4},{12,8},{16,12},{20,16},{24,20},{28,24},{32,28},{36,32}... | collective-permute-start | bytes 884744 | tf_op jit(solution)/shard_map/ppermute | solution.py:457
  29.4 8.9 %copy-start.2 = (f32[4,40]{1,0:T(4,128)S(1)}, f32[4,40]{1,0:T(4,128)}, u32[]{:S(2)}) copy-start(f32[4,40]{1,0:T(4,128)} %coup_ref.3) | copy-start | bytes 1924
  29.5 8.9 %copy-start.1 = (f32[40,40]{1,0:T(8,128)S(1)}, f32[40,40]{1,0:T(8,128)}, u32[]{:S(2)}) copy-start(f32[40,40]{1,0:T(8,128)} %block_ref.3) | copy-start | bytes 19204
  29.5 15.1 %collective-permute-start.2 = (f32[9,3,2,8,128]{4,3,2,1,0:T(8,128)S(1)}, f32[9,3,2,8,128]{4,3,2,1,0:T(8,128)S(1)}, u32[]{:S(2)}, u32[]{:S(2)}) collective-permute-start(f32[9,3,2,8,128]{4,3,2,1,0:T(8,128)S(1)} %get-tuple-element.51), channel_id=1, source_target_pairs={{0,1},{1,2},{2,3},{4,5},{5,6},{6,7},{8,9},{9,10},{10,11},{12,13},{... | collective-permute-start | bytes 663560 | tf_op jit(solution)/shard_map/ppermute | solution.py:457
  32.7 11.9 %collective-permute-start.3 = (f32[9,3,2,8,128]{4,3,2,1,0:T(8,128)S(1)}, f32[9,3,2,8,128]{4,3,2,1,0:T(8,128)S(1)}, u32[]{:S(2)}, u32[]{:S(2)}) collective-permute-start(f32[9,3,2,8,128]{4,3,2,1,0:T(8,128)S(1)} %get-tuple-element.50), channel_id=1, source_target_pairs={{1,0},{2,1},{3,2},{5,4},{6,5},{7,6},{9,8},{10,9},{11,10},{13,12},{... | collective-permute-start | bytes 663560 | tf_op jit(solution)/shard_map/ppermute | solution.py:457
  44.6 16.8 %all-to-all-start.1 = ((f32[4,26,16,128]{3,2,1,0:T(8,128)}), f32[4,26,16,128]{3,2,1,0:T(8,128)S(1)}, u32[]{:S(2)}, u32[]{:S(2)}) async-start(f32[4,26,16,128]{3,2,1,0:T(8,128)} %get-tuple-element.38), calls=%async_computation.1 | async-start | bytes 1703936 | tf_op jit(solution)/shard_map/all_to_all | solution.py:494
  49.8 32.4 %collective-permute-start.4 = (f32[9,10,8,128]{3,2,1,0:T(8,128)}, f32[9,10,8,128]{3,2,1,0:T(8,128)S(1)}, u32[]{:S(2)}, u32[]{:S(2)}) collective-permute-start(f32[9,10,8,128]{3,2,1,0:T(8,128)} %get-tuple-element.36), channel_id=1, source_target_pairs={{0,4},{4,8},{8,12},{12,16},{16,20},{20,24},{24,28},{28,32},{32,36}... | collective-permute-start | bytes 1105928 | tf_op jit(solution)/shard_map/ppermute | solution.py:457
  54.2 28.0 %collective-permute-start.5 = (f32[9,10,8,128]{3,2,1,0:T(8,128)}, f32[9,10,8,128]{3,2,1,0:T(8,128)S(1)}, u32[]{:S(2)}, u32[]{:S(2)}) collective-permute-start(f32[9,10,8,128]{3,2,1,0:T(8,128)} %get-tuple-element.37), channel_id=1, source_target_pairs={{4,0},{8,4},{12,8},{16,12},{20,16},{24,20},{28,24},{32,28},{36,32}... | collective-permute-start | bytes 1105928 | tf_op jit(solution)/shard_map/ppermute | solution.py:457
  64.0 34.7 %all-to-all-start.2 = ((f32[128,4,128]{2,1,0:T(4,128)}), f32[128,4,128]{2,1,0:T(4,128)S(1)}, u32[]{:S(2)}, u32[]{:S(2)}) async-start(f32[128,4,128]{2,1,0:T(4,128)} %get-tuple-element.46), calls=%async_computation.2 | async-start | bytes 524288 | tf_op jit(solution)/shard_map/all_to_all | solution.py:509
  76.9 7.1 %collective-permute-start.6 = (f32[16,8,128]{2,1,0:T(8,128)S(1)}, f32[16,8,128]{2,1,0:T(8,128)S(1)}, u32[]{:S(2)}, u32[]{:S(2)}) collective-permute-start(f32[16,8,128]{2,1,0:T(8,128)S(1)} %get-tuple-element.53), channel_id=1, source_target_pairs={{0,4},{4,8},{8,12},{12,16},{16,20},{20,24},{24,28},{28,32},{32,36}... | collective-permute-start | bytes 196616 | tf_op jit(solution)/shard_map/ppermute | solution.py:457
  80.2 9.2 %collective-permute-start.7 = (f32[16,8,128]{2,1,0:T(8,128)S(1)}, f32[16,8,128]{2,1,0:T(8,128)S(1)}, u32[]{:S(2)}, u32[]{:S(2)}) collective-permute-start(f32[16,8,128]{2,1,0:T(8,128)S(1)} %get-tuple-element.52), channel_id=1, source_target_pairs={{4,0},{8,4},{12,8},{16,12},{20,16},{24,20},{28,24},{32,28},{36,32}... | collective-permute-start | bytes 196616 | tf_op jit(solution)/shard_map/ppermute | solution.py:457
  91.1 7.6 %copy-start = (f32[40,2,768]{2,1,0:T(2,128)S(1)}, f32[40,2,768]{2,1,0:T(2,128)}, u32[]{:S(2)}) copy-start(f32[40,2,768]{2,1,0:T(2,128)} %a_ref.1) | copy-start | bytes 737284
  91.1 7.6 %copy-start.3 = (s32[768,1]{0,1:T(1,128)S(1)}, s32[768,1]{0,1:T(1,128)}, u32[]{:S(2)}) copy-start(s32[768,1]{0,1:T(1,128)} %param.12) | copy-start | bytes 9220
  91.1 7.6 %copy-start.4 = (s32[1,768]{1,0:T(1,128)S(1)}, s32[1,768]{1,0:T(1,128)}, u32[]{:S(2)}) copy-start(s32[1,768]{1,0:T(1,128)} %get-tuple-element.47.rank_ref) | copy-start | bytes 9220

commit v3 on v2

--- a/solution.py
+++ b/solution.py
@@ -74,7 +74,7 @@
     a_ref, tile_ref, spot_ref, block_ref, coup_ref, sems,
 ):
     pairs = (
-        (tile_hbm, tile_ref), (spot_hbm, spot_ref), (a_hbm, a_ref), (block_hbm, block_ref), (coup_hbm, coup_ref)
+        (tile_hbm, tile_ref), (spot_hbm, spot_ref), (block_hbm, block_ref), (coup_hbm, coup_ref), (a_hbm, a_ref)
     )
     copies = [pltpu.make_async_copy(src, dst, sems.at[i]) for i, (src, dst) in enumerate(pairs)]
     for copy in copies:
@@ -83,7 +83,11 @@
     tiles = msg_ref.shape[0]
     part = 256
     earlier = (iota((part, part), 0) < iota((part, part), 1)).astype(F32).astype(BF16)
-    copies[0].wait()
+    for copy in copies[:4]:
+        copy.wait()
+    c, b = coup_ref[...], block_ref[...]
+    cb = jnp.dot(c, b, precision=EXACT, preferred_element_type=F32)
+    cbb = jnp.dot(cb, b, precision=EXACT, preferred_element_type=F32)
     hot = (iota((tiles, count), 0) == tile_ref[...]).astype(F32)
     hot16 = hot.astype(BF16)
     ranks, seen = [], jnp.zeros((tiles, 1), F32)
@@ -93,12 +97,8 @@
         seen = seen + jnp.sum(chunk, axis=1, keepdims=True)
     rank = jnp.concatenate(ranks, axis=1).astype(jnp.int32)
     rank_ref[...] = rank
-    for copy in copies[1:]:
-        copy.wait()
+    copies[4].wait()
     a = jnp.concatenate([a_ref[:, 0, :], a_ref[:, 1, :]], axis=1)
-    c, b = coup_ref[...], block_ref[...]
-    cb = jnp.dot(c, b, precision=EXACT, preferred_element_type=F32)
-    cbb = jnp.dot(cb, b, precision=EXACT, preferred_element_type=F32)
     pad = jnp.zeros((12, 8), F32)
     w = jnp.concatenate([jnp.concatenate([c, cb, cbb], axis=0), pad], axis=1)
     a = jnp.concatenate([a, jnp.zeros((8, 2 * count), F32)], axis=0)
@@ -127,14 +127,16 @@
 CORNER = [(1, 1), (1, 2), (2, 1)]
 
 
-def pack_kernel(lo_ref, hi_ref, above_ref, below_ref, after_ref, up_ref, down_ref):
+def pack_kernel(x_ref, lo_ref, hi_ref, above_ref, below_ref, after_ref, up_ref, down_ref):
     for i, (k, d) in enumerate(CORNER):
         for j, (ref, l) in enumerate(((above_ref, 3 - k), (below_ref, k - 1))):
             up_ref[:, 3 * j + i] = ref[:, l, 2 - d]
             down_ref[:, 3 * j + i] = ref[:, l, d - 1]
     for l in range(4):
-        up_ref[:, 6 + l] = lo_ref[:, l, 1]
-        down_ref[:, 6 + l] = hi_ref[:, l, 0]
+        up_ref[:, 6 + l] = x_ref[:, l, 0]
+        down_ref[:, 6 + l] = x_ref[:, l, 1]
+        up_ref[:, 10 + l] = lo_ref[:, l]
+        down_ref[:, 10 + l] = hi_ref[:, l]
 
 
 def top_kernel(x_ref, lo_ref, hi_ref, coup_ref, block_ref, top_ref, mix_ref):
@@ -145,7 +147,7 @@
     mix_ref[1] = lax.dot_general(cb, c, nt, precision=EXACT, preferred_element_type=F32)
 
     def s0(l, r):
-        return (lo_ref[:, l, r + 2] if r < 0 else hi_ref[:, l, r - 2] if r > 1 else x_ref[:, l, r])
+        return lo_ref[:, l] if r < 0 else hi_ref[:, l] if r > 1 else x_ref[:, l, r]
 
     for r in range(2):
         rows = pl.ds(8 * r, 8)
@@ -160,7 +162,6 @@
         top_ref[0:8, rows, :] = first[0]
         top_ref[8:16, rows, :] = -2.0 * HOP * signed(first[1]) - s0(0, r)[:8]
         top_ref[16:25, rows, :] = s0(0, r)
-        top_ref[25:26, rows, :] = jnp.zeros((1, 8, 128), F32)
 
 
 def pure_kernel(
@@ -188,9 +189,9 @@
             return side[:, (0 if l < 0 else 3) + CORNER.index((k, d))]
         if k > 0:
             return above_ref[:, 3 - k, r] if l < 0 else below_ref[:, k - 1, r]
-        if d > 2:
-            return side[:, 6 + l]
-        return (lo_ref[:, l, r + 2] if r < 0 else hi_ref[:, l, r - 2] if r > 1 else x_ref[:, l, r])
+        if d > 1:
+            return side[:, 4 * d - 2 + l]
+        return lo_ref[:, l] if r < 0 else hi_ref[:, l] if r > 1 else x_ref[:, l, r]
 
     def s0(l, r):
         return start(l, r)[:8]
@@ -219,12 +220,20 @@
                 one_ref[:, l, r] = s
 
 
+def mix(k, s):
+    def row(o):
+        terms = [k[o : o + 1, q : q + 1] * s[2 * q : 2 * q + 2] for q in range(4)]
+        return (terms[0] + terms[1]) + (terms[2] + terms[3])
+
+    return jnp.concatenate([row(o) for o in range(4)], axis=0)
+
+
 def columns(got):
     width = got.shape[1] // 128
     return jnp.concatenate([got[:, 128 * j : 128 * (j + 1)].T for j in range(width)], axis=0)
 
 
-def scatter_kernel(pos_ref, got_ref, top_ref, out_ref, d2_ref, site_ref, dense_ref):
+def scatter_kernel(pos_ref, got_ref, top_ref, mix_ref, out_ref, d2_ref, site_ref, dense_ref):
     got = got_ref[:, 0, :]
     tiles = got.shape[0]
     slots = columns(got)
@@ -260,9 +269,13 @@
             k = k - k % 8 + (k % 2) * 4 + (k % 8) // 2
             return dense_ref[j, pl.ds(k, 8, stride=24), :]
 
+        number = dense_ref[j, 192:200, :]
+        d2_ref[8, rows, :] = number
+        mixed = mix(mix_ref[0], top_ref[16:24, rows, :])
         for k in range(8):
             q1 = dense(k) + jnp.where(on, top_ref[k, rows, :], 0.0)
-            q2 = 2.0 * dense(8 + k) + jnp.where(on, top_ref[8 + k, rows, :], 0.0)
+            q2 = top_ref[8 + k, rows, :] + 2.0 * (number * mixed[k])
+            q2 = 2.0 * dense(8 + k) + jnp.where(on, q2, 0.0)
             d2 = dense(16 + k)
             d2_ref[k, rows, :] = d2
             tail = jnp.where(on, top_ref[16 + k, rows, :], d2)
@@ -270,10 +283,9 @@
                 out_ref[y, k, rows, :] = q1
                 out_ref[y, 8 + k, rows, :] = q2
                 out_ref[y, 16 + k, rows, :] = tail
-        field = jnp.where(on, top_ref[24, rows, :], 0.0)
+        tail = jnp.where(on, top_ref[24, rows, :], number)
         for y in range(4):
-            out_ref[y, 24, rows, :] = field
-            out_ref[y, 25, rows, :] = dense_ref[j, 192:200, :]
+            out_ref[y, 24, rows, :] = tail
 
 
 def evolve_kernel(
@@ -284,13 +296,6 @@
     on = pos_ref[0] == 0
     kk, kb = mix_ref[0], mix_ref[1]
 
-    def mix(k, s):
-        def row(o):
-            terms = [k[o : o + 1, q : q + 1] * s[2 * q : 2 * q + 2] for q in range(4)]
-            return (terms[0] + terms[1]) + (terms[2] + terms[3])
-
-        return jnp.concatenate([row(o) for o in range(4)], axis=0)
-
     def rows_of(s):
         return s.reshape(s.shape[0], 2, 8, 128)
 
@@ -298,7 +303,7 @@
     field = rows_of(m_ref[0, 24:25])
     s1 = (m_ref[0, 0:8] + m_ref[1, 0:8]) + (m_ref[2, 0:8] + m_ref[3, 0:8])
     q2 = (m_ref[0, 8:16] + m_ref[1, 8:16]) + (m_ref[2, 8:16] + m_ref[3, 8:16])
-    number = (m_ref[0, 25:26] + m_ref[1, 25:26]) + (m_ref[2, 25:26] + m_ref[3, 25:26])
+    number = m_ref[1, 24:25] + m_ref[2, 24:25] + m_ref[3, 24:25]
 
     def flat_part(s):
         s = rows_of(s)
@@ -309,7 +314,8 @@
     s2 = hopped + 2.0 * flat_part(s1)
     d0 = jnp.where(on, s1 - top_ref[0:8], 0.0)
     delta = jnp.where(on, hopped - top_ref[8:16] + 2.0 * flat_part(d0), 0.0)
-    d2 = d2_ref[...] + (m_ref[1, 16:24] + m_ref[2, 16:24] + m_ref[3, 16:24])
+    number = number + d2_ref[8:9]
+    d2 = d2_ref[0:8] + (m_ref[1, 16:24] + m_ref[2, 16:24] + m_ref[3, 16:24])
     third = 2.0 * (d2 + number * (mix(kb, s0) + mix(kk, s1))) - d0
     d_ref[0:8] = d0
     d_ref[8:16] = delta
@@ -472,22 +478,23 @@
     x = jnp.concatenate(
         [substrate.reshape(8, 4, 2, 8, 128), disorder.reshape(1, 4, 2, 8, 128)], axis=0
     )
-    lo = shifted(x, "tile", tiles, 1)
-    hi = shifted(x, "tile", tiles, -1)
+    lo = shifted(x[:, :, 1], "tile", tiles, 1)
+    hi = shifted(x[:, :, 0], "tile", tiles, -1)
     above = shifted(x[:, 1:], "depth", depths, 1)
     below = shifted(x[:, :3], "depth", depths, -1)
-    top, mix = call(
-        top_kernel, "top", (shape(26, 16, 128), shape(2, 4, 4)), (x, lo, hi, coupling, adatom_block)
+    top, mix_products = call(
+        top_kernel, "top", (shape(25, 16, 128), shape(2, 4, 4)), (x, lo, hi, coupling, adatom_block),
+        cost=2*10**9,
     )
     part, d2, site = call(
         scatter_kernel, "scatter",
-        (shape(4, 26, 16, 128), shape(8, 16, 128), shape(48, tiles, dtype=jnp.int32)),
-        (pos, got, top),
+        (shape(4, 25, 16, 128), shape(9, 16, 128), shape(48, tiles, dtype=jnp.int32)),
+        (pos, got, top, mix_products),
         (pltpu.VMEM((2, 200, 128), F32),), smem=True,
     )
-    above, below, part = lax.optimization_barrier((above, below, part))
     up, down = call(
-        pack_kernel, "pack", (shape(9, 10, 8, 128), shape(9, 10, 8, 128)), (lo, hi, above, below, site)
+        pack_kernel, "pack", (shape(9, 14, 8, 128), shape(9, 14, 8, 128)), (x, lo, hi, above, below, site),
+        cost=10**10,
     )
     low2 = shifted(up, "tile", tiles, 1)
     high2 = shifted(down, "tile", tiles, -1)
@@ -495,7 +502,7 @@
     answer, d = call(
         evolve_kernel, "evolve",
         (shape(tiles, 4, 128), shape(24, 16, 128)),
-        (pos, part, top, d2, site, mix),
+        (pos, part, top, d2, site, mix_products),
         (pltpu.VMEM((384, 128), F32), pltpu.VMEM((128, 128), F32)), smem=True,
     )
     before = shifted(d[:16, 8:], "tile", tiles, 1)

time: 102 us -> 98.8 us (0.969)
  starting transfers between devices: 58.2 us -> 55.9 us
    all_to_all x1, starting transfers between devices: 12.8 us -> 10.4 us  [per_device(): lax.all_to_all(answer, 'tile', split_axis=0, concat_axis=0, tiled=True)]
    ppermute x8, waiting for transfers between devices: 9.72 us -> 7.91 us  [shifted(): return lax.ppermute(x, axis, pairs)]
    all_to_all x1, waiting for transfers between devices: 3.66 us -> 5.08 us  [per_device(): got = lax.all_to_all(msg, 'tile', split_axis=0, concat_axis=0, tiled=True)]
  transfers between devices with their start and end apart: 11 -> 11, of which waited for: 6 -> 5; matrix products, arithmetic and copies ran while one was open for 2% -> 2% of each run, Pallas kernels for 9% -> 9%
where the time goes in v3:
time: 98.8 us; the launch traced here: 97.8 us
  starting transfers between devices  55.9 us (57%)
  waiting for transfers between devices  24.7 us (25%)
  Pallas kernels  13.4 us (14%)
  local copies, waits for them, and re-layouts  2.78 us (3%)
    ppermute x8, starting transfers between devices, shifted(): return lax.ppermute(x, axis, pairs)  21.5 us
    all_to_all x1, starting transfers between devices, per_device(): got = lax.all_to_all(msg, 'tile', split_axis=0, concat_axis=0, tiled=True)  19.8 us
    pallas_call x8, Pallas kernels, call(): pl.pallas_call(kernel, out_shape=outs, in_specs=[SM if smem and i == 0 el...  13.4 us
    all_to_all x1, starting transfers between devices, per_device(): lax.all_to_all(answer, 'tile', split_axis=0, concat_axis=0, tiled=True)  10.4 us
    ppermute x8, waiting for transfers between devices, shifted(): return lax.ppermute(x, axis, pairs)  7.91 us
    all_to_all x1, waiting for transfers between devices, per_device(): lax.all_to_all(answer, 'tile', split_axis=0, concat_axis=0, tiled=True)  6.77 us
    all_to_all x1, waiting for transfers between devices, per_device(): got = lax.all_to_all(msg, 'tile', split_axis=0, concat_axis=0, tiled=True)  5.08 us
    all_to_all x1, waiting for transfers between devices, per_device(): lax.all_to_all(part, 'depth', split_axis=0, concat_axis=0, tiled=True)  4.94 us
  transfers between devices with their start and end apart: 11, of which 5 were waited for; matrix products, arithmetic and copies ran while one was open for 2% of the time, Pallas kernels for 9%

profile of v3, /device:TPU:7, one launch (start us, length us, event | category | flops | bytes accessed | tf_op | source)
XLA Modules:
  0.0 97.8 jit_solution(15521190208835349717)
XLA Ops:
  0.6 2.7 %route.1 = (f32[128,1,384]{2,1,0:T(1,128)}, s32[1,768]{1,0:T(1,128)}) custom-call(f32[40,2,768]{2,1,0:T(2,128)} %a_ref.1, s32[1,768]{1,0:T(1,128)} %bitcast.11, s32[768]{0:T(1024)} %spot_hbm.1, f32[40,40]{1,0:T(8,128)} %block_ref.3, f32[4,40]{1,0:T(4,128)} %coup_ref.3), custom_call_target="tpu_custom_call" | custom-call | tf_op jit(solution)/shard_map/route/pallas_call | solution.py:441
  3.3 0.0 copy-start.11
  3.3 19.8 %all-to-all-start = ((f32[128,1,384]{2,1,0:T(1,128)}), f32[128,1,384]{2,1,0:T(1,128)S(1)}, u32[]{:S(2)}, u32[]{:S(2)}) async-start(f32[128,1,384]{2,1,0:T(1,128)} %get-tuple-element.27), calls=%async_computation | async-start | bytes 393216 | tf_op jit(solution)/shard_map/all_to_all | solution.py:477
  23.2 0.0 copy-done.11
  23.2 0.2 reshape.24
  23.4 0.0 copy-start.12
  23.4 0.7 copy-done.12
  24.2 3.3 %collective-permute-start = (f32[9,4,8,128]{3,2,1,0:T(8,128)S(1)}, f32[9,4,8,128]{3,2,1,0:T(8,128)S(1)}, u32[]{:S(2)}, u32[]{:S(2)}) collective-permute-start(f32[9,4,8,128]{3,2,1,0:T(8,128)S(1)} %get-tuple-element.47), channel_id=1, source_target_pairs={{0,4},{4,8},{8,12},{12,16},{16,20},{20,24},{24,28},{28,32},{32,36}... | collective-permute-start | bytes 442376 | tf_op jit(solution)/shard_map/ppermute | solution.py:463
  27.6 1.9 %collective-permute-start.1 = (f32[9,4,8,128]{3,2,1,0:T(8,128)S(1)}, f32[9,4,8,128]{3,2,1,0:T(8,128)S(1)}, u32[]{:S(2)}, u32[]{:S(2)}) collective-permute-start(f32[9,4,8,128]{3,2,1,0:T(8,128)S(1)} %get-tuple-element.46), channel_id=1, source_target_pairs={{4,0},{8,4},{12,8},{16,12},{20,16},{24,20},{28,24},{32,28},{36,32}... | collective-permute-start | bytes 442376 | tf_op jit(solution)/shard_map/ppermute | solution.py:463
  29.5 0.0 copy-start.3
  29.6 0.0 copy-start.1
  29.6 3.2 %collective-permute-start.2 = (f32[9,3,2,8,128]{4,3,2,1,0:T(8,128)S(1)}, f32[9,3,2,8,128]{4,3,2,1,0:T(8,128)S(1)}, u32[]{:S(2)}, u32[]{:S(2)}) collective-permute-start(f32[9,3,2,8,128]{4,3,2,1,0:T(8,128)S(1)} %get-tuple-element.45), channel_id=1, source_target_pairs={{0,1},{1,2},{2,3},{4,5},{5,6},{6,7},{8,9},{9,10},{10,11},{12,13},{... | collective-permute-start | bytes 663560 | tf_op jit(solution)/shard_map/ppermute | solution.py:463
  32.8 1.3 %collective-permute-start.3 = (f32[9,3,2,8,128]{4,3,2,1,0:T(8,128)S(1)}, f32[9,3,2,8,128]{4,3,2,1,0:T(8,128)S(1)}, u32[]{:S(2)}, u32[]{:S(2)}) collective-permute-start(f32[9,3,2,8,128]{4,3,2,1,0:T(8,128)S(1)} %get-tuple-element.44), channel_id=1, source_target_pairs={{1,0},{2,1},{3,2},{5,4},{6,5},{7,6},{9,8},{10,9},{11,10},{13,12},{... | collective-permute-start | bytes 663560 | tf_op jit(solution)/shard_map/ppermute | solution.py:463
  34.1 0.1 pad_add_fusion.pos_ref
  34.2 0.0 collective-permute-done.lo_ref
  34.2 0.0 copy-start.7
  34.2 2.6 %collective-permute-done.1.hi_ref = f32[9,4,8,128]{3,2,1,0:T(8,128)S(1)} collective-permute-done((f32[9,4,8,128]{3,2,1,0:T(8,128)S(1)}, f32[9,4,8,128]{3,2,1,0:T(8,128)S(1)}, u32[]{:S(2)}, u32[]{:S(2)}) %collective-permute-start.1) | collective-permute-done | bytes 147488 | tf_op jit(solution)/shard_map/ppermute | solution.py:463
  36.8 0.0 copy-done.3
  36.8 0.0 copy-done.1
  36.8 0.0 copy-start.9
  36.8 0.3 top.1
  37.1 5.1 %all-to-all-done.got_ref = f32[128,1,384]{2,1,0:T(1,128)S(1)} async-done(((f32[128,1,384]{2,1,0:T(1,128)}), f32[128,1,384]{2,1,0:T(1,128)S(1)}, u32[]{:S(2)}, u32[]{:S(2)}) %all-to-all-start) | async-done | bytes 196640 | tf_op jit(solution)/shard_map/all_to_all | solution.py:477
  42.2 2.3 %scatter.1 = (f32[4,25,16,128]{3,2,1,0:T(8,128)}, f32[9,16,128]{2,1,0:T(8,128)S(1)}, s32[48,128]{1,0:T(8,128)S(1)}) custom-call(s32[4]{0:T(128)S(1)} %pad_add_fusion.pos_ref, f32[128,1,384]{2,1,0:T(1,128)S(1)} %all-to-all-done.got_ref, f32[25,16,128]{2,1,0:T(8,128)S(1)} %get-tuple-element.28.top_ref, f32[2,4,4]{2,1,0:T(4,128)S(1)} %get-tuple-element.29.mix_ref), custom_call_target="tpu_custom_call" | custom-call | tf_op jit(solution)/shard_map/scatter/pallas_call | solution.py:441
  44.5 4.2 %all-to-all-start.1 = ((f32[4,25,16,128]{3,2,1,0:T(8,128)}), f32[4,25,16,128]{3,2,1,0:T(8,128)S(1)}, u32[]{:S(2)}, u32[]{:S(2)}) async-start(f32[4,25,16,128]{3,2,1,0:T(8,128)} %get-tuple-element.33), calls=%async_computation.1 | async-start | bytes 1638400 | tf_op jit(solution)/shard_map/all_to_all | solution.py:501
  48.7 0.0 collective-permute-done.2.above_ref
  48.7 0.0 collective-permute-done.3.below_ref
  48.7 0.0 copy-start.5
  48.7 0.0 copy-done.7
  48.7 0.0 copy-done.9
  48.7 0.9 pack.1
  49.6 0.0 copy-done.5
  49.6 4.4 %collective-permute-start.4 = (f32[9,14,8,128]{3,2,1,0:T(8,128)}, f32[9,14,8,128]{3,2,1,0:T(8,128)S(1)}, u32[]{:S(2)}, u32[]{:S(2)}) collective-permute-start(f32[9,14,8,128]{3,2,1,0:T(8,128)} %get-tuple-element.31), channel_id=1, source_target_pairs={{0,4},{4,8},{8,12},{12,16},{16,20},{20,24},{24,28},{28,32},{32,36}... | collective-permute-start | bytes 1548296 | tf_op jit(solution)/shard_map/ppermute | solution.py:463
  54.0 1.9 %collective-permute-start.5 = (f32[9,14,8,128]{3,2,1,0:T(8,128)S(1)}, f32[9,14,8,128]{3,2,1,0:T(8,128)S(1)}, u32[]{:S(2)}, u32[]{:S(2)}) collective-permute-start(f32[9,14,8,128]{3,2,1,0:T(8,128)S(1)} %get-tuple-element.32), channel_id=1, source_target_pairs={{4,0},{8,4},{12,8},{16,12},{20,16},{24,20},{28,24},{32,28},{36,32}... | collective-permute-start | bytes 1548296 | tf_op jit(solution)/shard_map/ppermute | solution.py:463
  55.9 4.9 %all-to-all-done.1.m_ref = f32[4,25,16,128]{3,2,1,0:T(8,128)S(1)} async-done(((f32[4,25,16,128]{3,2,1,0:T(8,128)}), f32[4,25,16,128]{3,2,1,0:T(8,128)S(1)}, u32[]{:S(2)}, u32[]{:S(2)}) %all-to-all-start.1) | async-done | bytes 819232 | tf_op jit(solution)/shard_map/all_to_all | solution.py:501
  60.9 2.6 %evolve.1 = (f32[128,4,128]{2,1,0:T(4,128)}, f32[24,16,128]{2,1,0:T(8,128)S(1)}) custom-call(s32[4]{0:T(128)S(1)} %pad_add_fusion.pos_ref, f32[4,25,16,128]{3,2,1,0:T(8,128)S(1)} %all-to-all-done.1.m_ref, f32[25,16,128]{2,1,0:T(8,128)S(1)} %get-tuple-element.28.top_ref, f32[9,16,128]{2,1,0:T(8,128)S(1)} %get-tuple-element.34.d2_ref, ...), custom_call_target="tpu_custom_call" | custom-call | tf_op jit(solution)/shard_map/evolve/pallas_call | solution.py:441
  63.5 0.0 copy-start.8
  63.5 0.0 copy-start.10
  63.5 10.4 %all-to-all-start.2 = ((f32[128,4,128]{2,1,0:T(4,128)}), f32[128,4,128]{2,1,0:T(4,128)S(1)}, u32[]{:S(2)}, u32[]{:S(2)}) async-start(f32[128,4,128]{2,1,0:T(4,128)} %get-tuple-element.40), calls=%async_computation.2 | async-start | bytes 524288 | tf_op jit(solution)/shard_map/all_to_all | solution.py:516
  73.9 0.0 copy-start.6
  73.9 3.5 %collective-permute-start.6 = (f32[16,8,128]{2,1,0:T(8,128)S(1)}, f32[16,8,128]{2,1,0:T(8,128)S(1)}, u32[]{:S(2)}, u32[]{:S(2)}) collective-permute-start(f32[16,8,128]{2,1,0:T(8,128)S(1)} %get-tuple-element.49), channel_id=1, source_target_pairs={{0,4},{4,8},{8,12},{12,16},{16,20},{20,24},{24,28},{28,32},{32,36}... | collective-permute-start | bytes 196616 | tf_op jit(solution)/shard_map/ppermute | solution.py:463
  77.4 1.9 %collective-permute-start.7 = (f32[16,8,128]{2,1,0:T(8,128)S(1)}, f32[16,8,128]{2,1,0:T(8,128)S(1)}, u32[]{:S(2)}, u32[]{:S(2)}) collective-permute-start(f32[16,8,128]{2,1,0:T(8,128)S(1)} %get-tuple-element.48), channel_id=1, source_target_pairs={{4,0},{8,4},{12,8},{16,12},{20,16},{24,20},{28,24},{32,28},{36,32}... | collective-permute-start | bytes 196616 | tf_op jit(solution)/shard_map/ppermute | solution.py:463
  79.3 0.0 collective-permute-done.4.low2_ref
  79.3 0.0 collective-permute-done.5.high2_ref
  79.3 0.0 copy-done.8
  79.4 0.0 copy-done.10
  79.4 0.0 copy-done.6
  79.4 1.8 %pure.1 = (f32[8,4,2,8,128]{4,3,2,1,0:T(8,128)S(1)}, f32[8,6,4,8,128]{4,3,2,1,0:T(8,128)S(1)}) custom-call(s32[4]{0:T(128)S(1)} %pad_add_fusion.pos_ref, f32[9,4,2,8,128]{4,3,2,1,0:T(8,128)S(1)} %constant_dynamic-update-slice_fusion.x_ref, f32[9,4,8,128]{3,2,1,0:T(8,128)S(1)} %copy-done.8, f32[9,4,8,128]{3,2,1,0:T(8,128)S(1)} %copy-done.10, ...), custom_call_target="tpu_custom_call" | custom-call | flops 10000000000 | tf_op jit(solution)/shard_map/pure/pallas_call | solution.py:441
  81.2 0.0 collective-permute-done.6.before_ref
  81.2 5.3 %collective-permute-done.7.after_ref = f32[16,8,128]{2,1,0:T(8,128)S(1)} collective-permute-done((f32[16,8,128]{2,1,0:T(8,128)S(1)}, f32[16,8,128]{2,1,0:T(8,128)S(1)}, u32[]{:S(2)}, u32[]{:S(2)}) %collective-permute-start.7) | collective-permute-done | bytes 65568 | tf_op jit(solution)/shard_map/ppermute | solution.py:463
  86.5 0.8 last.1
  87.3 0.8 reshape.26
  88.1 0.0 copy-start
  88.1 0.0 copy-start.2
  88.1 0.0 copy-start.4
  88.1 0.8 reshape.27
  89.0 6.8 %all-to-all-done.2.back_ref = f32[128,4,128]{2,1,0:T(4,128)S(1)} async-done(((f32[128,4,128]{2,1,0:T(4,128)}), f32[128,4,128]{2,1,0:T(4,128)S(1)}, u32[]{:S(2)}, u32[]{:S(2)}) %all-to-all-start.2) | async-done | bytes 262176 | tf_op jit(solution)/shard_map/all_to_all | solution.py:516
  95.8 0.0 copy-done
  95.8 0.0 copy-done.2
  95.8 0.0 copy-done.4
  95.8 2.0 %adatoms.1 = (f32[40,2,768]{2,1,0:T(2,128)}, f32[40,2,768]{2,1,0:T(2,128)}) custom-call(f32[40,2,768]{2,1,0:T(2,128)S(1)} %copy-done, f32[128,4,128]{2,1,0:T(4,128)S(1)} %all-to-all-done.2.back_ref, s32[1,768]{1,0:T(1,128)S(1)} %bitcast.12, s32[1,768]{1,0:T(1,128)S(1)} %copy-done.4, f32[40,40]{1,0:T(8,128)S(1)} %copy-done.1, f32[4,40]{1,0:T(4,128)S(1)} %copy-done.3), custom_call_target="tpu_custom_call" | custom-call | tf_op jit(solution)/shard_map/adatoms/pallas_call | solution.py:441
  (6 shorter events, 0.1 us)
Async XLA Ops:
  3.3 19.8 %copy-start.11 = (f32[4,2,4,2,1024]{4,3,2,1,0:T(2,128)S(1)}, f32[4,2,4,2,1024]{4,3,2,1,0:T(2,128)}, u32[]{:S(2)}) copy-start(f32[4,2,4,2,1024]{4,3,2,1,0:T(2,128)} %param.7) | copy-start | bytes 786436
  3.3 38.8 %all-to-all-start = ((f32[128,1,384]{2,1,0:T(1,128)}), f32[128,1,384]{2,1,0:T(1,128)S(1)}, u32[]{:S(2)}, u32[]{:S(2)}) async-start(f32[128,1,384]{2,1,0:T(1,128)} %get-tuple-element.27), calls=%async_computation | async-start | bytes 393216 | tf_op jit(solution)/shard_map/all_to_all | solution.py:477
  23.4 0.8 copy-start.12
  24.2 9.9 %collective-permute-start = (f32[9,4,8,128]{3,2,1,0:T(8,128)S(1)}, f32[9,4,8,128]{3,2,1,0:T(8,128)S(1)}, u32[]{:S(2)}, u32[]{:S(2)}) collective-permute-start(f32[9,4,8,128]{3,2,1,0:T(8,128)S(1)} %get-tuple-element.47), channel_id=1, source_target_pairs={{0,4},{4,8},{8,12},{12,16},{16,20},{20,24},{24,28},{28,32},{32,36}... | collective-permute-start | bytes 442376 | tf_op jit(solution)/shard_map/ppermute | solution.py:463
  27.6 9.2 %collective-permute-start.1 = (f32[9,4,8,128]{3,2,1,0:T(8,128)S(1)}, f32[9,4,8,128]{3,2,1,0:T(8,128)S(1)}, u32[]{:S(2)}, u32[]{:S(2)}) collective-permute-start(f32[9,4,8,128]{3,2,1,0:T(8,128)S(1)} %get-tuple-element.46), channel_id=1, source_target_pairs={{4,0},{8,4},{12,8},{16,12},{20,16},{24,20},{28,24},{32,28},{36,32}... | collective-permute-start | bytes 442376 | tf_op jit(solution)/shard_map/ppermute | solution.py:463
  29.5 7.3 %copy-start.3 = (f32[4,40]{1,0:T(4,128)S(1)}, f32[4,40]{1,0:T(4,128)}, u32[]{:S(2)}) copy-start(f32[4,40]{1,0:T(4,128)} %coup_ref.3) | copy-start | bytes 1924
  29.6 7.2 %copy-start.1 = (f32[40,40]{1,0:T(8,128)S(1)}, f32[40,40]{1,0:T(8,128)}, u32[]{:S(2)}) copy-start(f32[40,40]{1,0:T(8,128)} %block_ref.3) | copy-start | bytes 19204
  29.6 19.1 %collective-permute-start.2 = (f32[9,3,2,8,128]{4,3,2,1,0:T(8,128)S(1)}, f32[9,3,2,8,128]{4,3,2,1,0:T(8,128)S(1)}, u32[]{:S(2)}, u32[]{:S(2)}) collective-permute-start(f32[9,3,2,8,128]{4,3,2,1,0:T(8,128)S(1)} %get-tuple-element.45), channel_id=1, source_target_pairs={{0,1},{1,2},{2,3},{4,5},{5,6},{6,7},{8,9},{9,10},{10,11},{12,13},{... | collective-permute-start | bytes 663560 | tf_op jit(solution)/shard_map/ppermute | solution.py:463
  32.8 15.9 %collective-permute-start.3 = (f32[9,3,2,8,128]{4,3,2,1,0:T(8,128)S(1)}, f32[9,3,2,8,128]{4,3,2,1,0:T(8,128)S(1)}, u32[]{:S(2)}, u32[]{:S(2)}) collective-permute-start(f32[9,3,2,8,128]{4,3,2,1,0:T(8,128)S(1)} %get-tuple-element.44), channel_id=1, source_target_pairs={{1,0},{2,1},{3,2},{5,4},{6,5},{7,6},{9,8},{10,9},{11,10},{13,12},{... | collective-permute-start | bytes 663560 | tf_op jit(solution)/shard_map/ppermute | solution.py:463
  34.2 14.5 %copy-start.7 = (f32[9,4,8,128]{3,2,1,0:T(8,128)}, f32[9,4,8,128]{3,2,1,0:T(8,128)S(1)}, u32[]{:S(2)}) copy-start(f32[9,4,8,128]{3,2,1,0:T(8,128)S(1)} %collective-permute-done.lo_ref) | copy-start | bytes 442372
  36.8 11.9 %copy-start.9 = (f32[9,4,8,128]{3,2,1,0:T(8,128)}, f32[9,4,8,128]{3,2,1,0:T(8,128)S(1)}, u32[]{:S(2)}) copy-start(f32[9,4,8,128]{3,2,1,0:T(8,128)S(1)} %collective-permute-done.1.hi_ref) | copy-start | bytes 442372
  44.5 16.4 %all-to-all-start.1 = ((f32[4,25,16,128]{3,2,1,0:T(8,128)}), f32[4,25,16,128]{3,2,1,0:T(8,128)S(1)}, u32[]{:S(2)}, u32[]{:S(2)}) async-start(f32[4,25,16,128]{3,2,1,0:T(8,128)} %get-tuple-element.33), calls=%async_computation.1 | async-start | bytes 1638400 | tf_op jit(solution)/shard_map/all_to_all | solution.py:501
  48.7 0.9 copy-start.5
  49.6 29.7 %collective-permute-start.4 = (f32[9,14,8,128]{3,2,1,0:T(8,128)}, f32[9,14,8,128]{3,2,1,0:T(8,128)S(1)}, u32[]{:S(2)}, u32[]{:S(2)}) collective-permute-start(f32[9,14,8,128]{3,2,1,0:T(8,128)} %get-tuple-element.31), channel_id=1, source_target_pairs={{0,4},{4,8},{8,12},{12,16},{16,20},{20,24},{24,28},{28,32},{32,36}... | collective-permute-start | bytes 1548296 | tf_op jit(solution)/shard_map/ppermute | solution.py:463
  54.0 25.3 %collective-permute-start.5 = (f32[9,14,8,128]{3,2,1,0:T(8,128)S(1)}, f32[9,14,8,128]{3,2,1,0:T(8,128)S(1)}, u32[]{:S(2)}, u32[]{:S(2)}) collective-permute-start(f32[9,14,8,128]{3,2,1,0:T(8,128)S(1)} %get-tuple-element.32), channel_id=1, source_target_pairs={{4,0},{8,4},{12,8},{16,12},{20,16},{24,20},{28,24},{32,28},{36,32}... | collective-permute-start | bytes 1548296 | tf_op jit(solution)/shard_map/ppermute | solution.py:463
  63.5 15.8 %copy-start.8 = (f32[9,4,8,128]{3,2,1,0:T(8,128)S(1)}, f32[9,4,8,128]{3,2,1,0:T(8,128)}, u32[]{:S(2)}) copy-start(f32[9,4,8,128]{3,2,1,0:T(8,128)} %copy-done.7) | copy-start | bytes 442372
  63.5 15.9 %copy-start.10 = (f32[9,4,8,128]{3,2,1,0:T(8,128)S(1)}, f32[9,4,8,128]{3,2,1,0:T(8,128)}, u32[]{:S(2)}) copy-start(f32[9,4,8,128]{3,2,1,0:T(8,128)} %copy-done.9) | copy-start | bytes 442372
  63.5 32.2 %all-to-all-start.2 = ((f32[128,4,128]{2,1,0:T(4,128)}), f32[128,4,128]{2,1,0:T(4,128)S(1)}, u32[]{:S(2)}, u32[]{:S(2)}) async-start(f32[128,4,128]{2,1,0:T(4,128)} %get-tuple-element.40), calls=%async_computation.2 | async-start | bytes 524288 | tf_op jit(solution)/shard_map/all_to_all | solution.py:516
  73.9 5.5 %copy-start.6 = (f32[9,3,2,8,128]{4,3,2,1,0:T(8,128)S(1)}, f32[9,3,2,8,128]{4,3,2,1,0:T(8,128)}, u32[]{:S(2)}) copy-start(f32[9,3,2,8,128]{4,3,2,1,0:T(8,128)} %copy-done.5) | copy-start | bytes 663556
  73.9 7.3 %collective-permute-start.6 = (f32[16,8,128]{2,1,0:T(8,128)S(1)}, f32[16,8,128]{2,1,0:T(8,128)S(1)}, u32[]{:S(2)}, u32[]{:S(2)}) collective-permute-start(f32[16,8,128]{2,1,0:T(8,128)S(1)} %get-tuple-element.49), channel_id=1, source_target_pairs={{0,4},{4,8},{8,12},{12,16},{16,20},{20,24},{24,28},{28,32},{32,36}... | collective-permute-start | bytes 196616 | tf_op jit(solution)/shard_map/ppermute | solution.py:463
  77.4 9.1 %collective-permute-start.7 = (f32[16,8,128]{2,1,0:T(8,128)S(1)}, f32[16,8,128]{2,1,0:T(8,128)S(1)}, u32[]{:S(2)}, u32[]{:S(2)}) collective-permute-start(f32[16,8,128]{2,1,0:T(8,128)S(1)} %get-tuple-element.48), channel_id=1, source_target_pairs={{4,0},{8,4},{12,8},{16,12},{20,16},{24,20},{28,24},{32,28},{36,32}... | collective-permute-start | bytes 196616 | tf_op jit(solution)/shard_map/ppermute | solution.py:463
  88.1 7.6 %copy-start = (f32[40,2,768]{2,1,0:T(2,128)S(1)}, f32[40,2,768]{2,1,0:T(2,128)}, u32[]{:S(2)}) copy-start(f32[40,2,768]{2,1,0:T(2,128)} %a_ref.1) | copy-start | bytes 737284
  88.1 7.6 %copy-start.2 = (s32[768,1]{0,1:T(1,128)S(1)}, s32[768,1]{0,1:T(1,128)}, u32[]{:S(2)}) copy-start(s32[768,1]{0,1:T(1,128)} %param.12) | copy-start | bytes 9220
  88.1 7.6 %copy-start.4 = (s32[1,768]{1,0:T(1,128)S(1)}, s32[1,768]{1,0:T(1,128)}, u32[]{:S(2)}) copy-start(s32[1,768]{1,0:T(1,128)} %get-tuple-element.41.rank_ref) | copy-start | bytes 9220

commit v4 on v3

--- a/solution.py
+++ b/solution.py
@@ -135,8 +135,10 @@
     for l in range(4):
         up_ref[:, 6 + l] = x_ref[:, l, 0]
         down_ref[:, 6 + l] = x_ref[:, l, 1]
-        up_ref[:, 10 + l] = lo_ref[:, l]
-        down_ref[:, 10 + l] = hi_ref[:, l]
+        up_ref[0:8, 10 + l] = lo_ref[:, l]
+        down_ref[0:8, 10 + l] = hi_ref[:, l]
+        up_ref[8:9, 10 + l] = x_ref[8:9, l, 1]
+        down_ref[8:9, 10 + l] = x_ref[8:9, l, 0]
 
 
 def top_kernel(x_ref, lo_ref, hi_ref, coup_ref, block_ref, top_ref, mix_ref):
@@ -196,6 +198,11 @@
     def s0(l, r):
         return start(l, r)[:8]
 
+    def potential(l, r):
+        if 0 <= l < 4 and r in (-1, 2):
+            return (low2_ref if r < 0 else high2_ref)[8:9, 10 + l]
+        return start(l, r)[8:9]
+
     def beyond(l, r):
         return max(-l, l - 3, 0) + max(-r, r - 1, 0)
 
@@ -203,10 +210,9 @@
         for r in range(-2, 4):
             if beyond(l, r) > 2:
                 continue
-            here = start(l, r)
-            s = here[:8]
+            s = s0(l, r)
             around = beside(s) + s0(l - 1, r) + s0(l + 1, r) + s0(l, r - 1) + s0(l, r + 1)
-            s1_ref[:, l + 2, r + 2] = masked(local_part(s, here[8:9], around), l, r)
+            s1_ref[:, l + 2, r + 2] = masked(local_part(s, potential(l, r), around), l, r)
     for l in range(-1, 5):
         for r in range(-1, 3):
             if beyond(l, r) > 1:
@@ -214,7 +220,7 @@
             s = s1_ref[:, l + 2, r + 2]
             around = beside(s) + s1_ref[:, l + 1, r + 2] + s1_ref[:, l + 3, r + 2]
             around = around + s1_ref[:, l + 2, r + 1] + s1_ref[:, l + 2, r + 3]
-            new = 2.0 * local_part(s, start(l, r)[8:9], around) - s0(l, r)
+            new = 2.0 * local_part(s, potential(l, r), around) - s0(l, r)
             two_ref[:, l + 1, r + 1] = masked(new, l, r)
             if beyond(l, r) == 0:
                 one_ref[:, l, r] = s
@@ -475,11 +481,10 @@
     )
     substrate, disorder, rank = lax.optimization_barrier((substrate_start, disorder, rank))
     got = lax.all_to_all(msg, "tile", split_axis=0, concat_axis=0, tiled=True)
-    x = jnp.concatenate(
-        [substrate.reshape(8, 4, 2, 8, 128), disorder.reshape(1, 4, 2, 8, 128)], axis=0
-    )
-    lo = shifted(x[:, :, 1], "tile", tiles, 1)
-    hi = shifted(x[:, :, 0], "tile", tiles, -1)
+    substrate = substrate.reshape(8, 4, 2, 8, 128)
+    lo = shifted(substrate[:, :, 1], "tile", tiles, 1)
+    hi = shifted(substrate[:, :, 0], "tile", tiles, -1)
+    x = jnp.concatenate([substrate, disorder.reshape(1, 4, 2, 8, 128)], axis=0)
     above = shifted(x[:, 1:], "depth", depths, 1)
     below = shifted(x[:, :3], "depth", depths, -1)
     top, mix_products = call(

time: 98.8 us -> 97.8 us (0.990)
  starting transfers between devices: 55.9 us -> 54.9 us
where the time goes in v4:
time: 97.8 us; the launch traced here: 96.8 us
  starting transfers between devices  54.9 us (56%)
  waiting for transfers between devices  25.4 us (26%)
  Pallas kernels  13.4 us (14%)
  local copies, waits for them, and re-layouts  2.05 us (2%)
    ppermute x8, starting transfers between devices, shifted(): return lax.ppermute(x, axis, pairs)  21.5 us
    all_to_all x1, starting transfers between devices, per_device(): got = lax.all_to_all(msg, 'tile', split_axis=0, concat_axis=0, tiled=True)  19.8 us
    pallas_call x8, Pallas kernels, call(): pl.pallas_call(kernel, out_shape=outs, in_specs=[SM if smem and i == 0 el...  13.4 us
    all_to_all x1, starting transfers between devices, per_device(): lax.all_to_all(answer, 'tile', split_axis=0, concat_axis=0, tiled=True)  9.4 us
    ppermute x8, waiting for transfers between devices, shifted(): return lax.ppermute(x, axis, pairs)  7.97 us
    all_to_all x1, waiting for transfers between devices, per_device(): lax.all_to_all(answer, 'tile', split_axis=0, concat_axis=0, tiled=True)  6.77 us
    all_to_all x1, waiting for transfers between devices, per_device(): got = lax.all_to_all(msg, 'tile', split_axis=0, concat_axis=0, tiled=True)  5.72 us
    all_to_all x1, waiting for transfers between devices, per_device(): lax.all_to_all(part, 'depth', split_axis=0, concat_axis=0, tiled=True)  4.95 us
  transfers between devices with their start and end apart: 11, of which 5 were waited for; matrix products, arithmetic and copies ran while one was open for 2% of the time, Pallas kernels for 9%

profile of v4, /device:TPU:7, one launch (start us, length us, event | category | flops | bytes accessed | tf_op | source)
XLA Modules:
  0.0 96.8 jit_solution(4736951227595310388)
XLA Ops:
  0.6 2.7 %route.1 = (f32[128,1,384]{2,1,0:T(1,128)}, s32[1,768]{1,0:T(1,128)}) custom-call(f32[40,2,768]{2,1,0:T(2,128)} %a_ref.1, s32[1,768]{1,0:T(1,128)} %bitcast.11, s32[768]{0:T(1024)} %spot_hbm.1, f32[40,40]{1,0:T(8,128)} %block_ref.3, f32[4,40]{1,0:T(4,128)} %coup_ref.3), custom_call_target="tpu_custom_call" | custom-call | tf_op jit(solution)/shard_map/route/pallas_call | solution.py:447
  3.3 0.0 copy-start.9
  3.3 19.8 %all-to-all-start = ((f32[128,1,384]{2,1,0:T(1,128)}), f32[128,1,384]{2,1,0:T(1,128)S(1)}, u32[]{:S(2)}, u32[]{:S(2)}) async-start(f32[128,1,384]{2,1,0:T(1,128)} %get-tuple-element.27), calls=%async_computation | async-start | bytes 393216 | tf_op jit(solution)/shard_map/all_to_all | solution.py:483
  23.2 0.0 copy-done.9
  23.2 0.2 reshape.24
  23.4 0.0 copy-start.10
  23.4 3.3 %collective-permute-start = (f32[8,4,8,128]{3,2,1,0:T(8,128)S(1)}, f32[8,4,8,128]{3,2,1,0:T(8,128)S(1)}, u32[]{:S(2)}, u32[]{:S(2)}) collective-permute-start(f32[8,4,8,128]{3,2,1,0:T(8,128)S(1)} %get-tuple-element.47), channel_id=1, source_target_pairs={{0,4},{4,8},{8,12},{12,16},{16,20},{20,24},{24,28},{28,32},{32,36}... | collective-permute-start | bytes 393224 | tf_op jit(solution)/shard_map/ppermute | solution.py:469
  26.8 1.9 %collective-permute-start.1 = (f32[8,4,8,128]{3,2,1,0:T(8,128)S(1)}, f32[8,4,8,128]{3,2,1,0:T(8,128)S(1)}, u32[]{:S(2)}, u32[]{:S(2)}) collective-permute-start(f32[8,4,8,128]{3,2,1,0:T(8,128)S(1)} %get-tuple-element.46), channel_id=1, source_target_pairs={{4,0},{8,4},{12,8},{16,12},{20,16},{24,20},{28,24},{32,28},{36,32}... | collective-permute-start | bytes 393224 | tf_op jit(solution)/shard_map/ppermute | solution.py:469
  28.7 0.0 copy-done.10
  28.8 0.0 copy-start.3
  28.9 0.0 copy-start.1
  28.9 3.2 %collective-permute-start.2 = (f32[9,3,2,8,128]{4,3,2,1,0:T(8,128)S(1)}, f32[9,3,2,8,128]{4,3,2,1,0:T(8,128)S(1)}, u32[]{:S(2)}, u32[]{:S(2)}) collective-permute-start(f32[9,3,2,8,128]{4,3,2,1,0:T(8,128)S(1)} %get-tuple-element.45), channel_id=1, source_target_pairs={{0,1},{1,2},{2,3},{4,5},{5,6},{6,7},{8,9},{9,10},{10,11},{12,13},{... | collective-permute-start | bytes 663560 | tf_op jit(solution)/shard_map/ppermute | solution.py:469
  32.1 1.3 %collective-permute-start.3 = (f32[9,3,2,8,128]{4,3,2,1,0:T(8,128)S(1)}, f32[9,3,2,8,128]{4,3,2,1,0:T(8,128)S(1)}, u32[]{:S(2)}, u32[]{:S(2)}) collective-permute-start(f32[9,3,2,8,128]{4,3,2,1,0:T(8,128)S(1)} %get-tuple-element.44), channel_id=1, source_target_pairs={{1,0},{2,1},{3,2},{5,4},{6,5},{7,6},{9,8},{10,9},{11,10},{13,12},{... | collective-permute-start | bytes 663560 | tf_op jit(solution)/shard_map/ppermute | solution.py:469
  33.4 0.1 pad_add_fusion.pos_ref
  33.5 0.0 collective-permute-done.lo_ref
  33.5 2.7 %collective-permute-done.1.hi_ref = f32[8,4,8,128]{3,2,1,0:T(8,128)S(1)} collective-permute-done((f32[8,4,8,128]{3,2,1,0:T(8,128)S(1)}, f32[8,4,8,128]{3,2,1,0:T(8,128)S(1)}, u32[]{:S(2)}, u32[]{:S(2)}) %collective-permute-start.1) | collective-permute-done | bytes 131104 | tf_op jit(solution)/shard_map/ppermute | solution.py:469
  36.2 0.0 copy-done.3
  36.2 0.0 copy-done.1
  36.2 0.0 copy-start.7
  36.2 0.3 top.1
  36.5 5.7 %all-to-all-done.got_ref = f32[128,1,384]{2,1,0:T(1,128)S(1)} async-done(((f32[128,1,384]{2,1,0:T(1,128)}), f32[128,1,384]{2,1,0:T(1,128)S(1)}, u32[]{:S(2)}, u32[]{:S(2)}) %all-to-all-start) | async-done | bytes 196640 | tf_op jit(solution)/shard_map/all_to_all | solution.py:483
  42.2 2.3 %scatter.1 = (f32[4,25,16,128]{3,2,1,0:T(8,128)}, f32[9,16,128]{2,1,0:T(8,128)S(1)}, s32[48,128]{1,0:T(8,128)S(1)}) custom-call(s32[4]{0:T(128)S(1)} %pad_add_fusion.pos_ref, f32[128,1,384]{2,1,0:T(1,128)S(1)} %all-to-all-done.got_ref, f32[25,16,128]{2,1,0:T(8,128)S(1)} %get-tuple-element.28.top_ref, f32[2,4,4]{2,1,0:T(4,128)S(1)} %get-tuple-element.29.mix_ref), custom_call_target="tpu_custom_call" | custom-call | tf_op jit(solution)/shard_map/scatter/pallas_call | solution.py:447
  44.5 4.2 %all-to-all-start.1 = ((f32[4,25,16,128]{3,2,1,0:T(8,128)}), f32[4,25,16,128]{3,2,1,0:T(8,128)S(1)}, u32[]{:S(2)}, u32[]{:S(2)}) async-start(f32[4,25,16,128]{3,2,1,0:T(8,128)} %get-tuple-element.33), calls=%async_computation.1 | async-start | bytes 1638400 | tf_op jit(solution)/shard_map/all_to_all | solution.py:506
  48.7 0.0 collective-permute-done.2.above_ref
  48.7 0.0 collective-permute-done.3.below_ref
  48.7 0.0 copy-start.5
  48.7 0.0 copy-done.7
  48.7 0.9 pack.1
  49.6 0.0 copy-done.5
  49.6 4.4 %collective-permute-start.4 = (f32[9,14,8,128]{3,2,1,0:T(8,128)}, f32[9,14,8,128]{3,2,1,0:T(8,128)S(1)}, u32[]{:S(2)}, u32[]{:S(2)}) collective-permute-start(f32[9,14,8,128]{3,2,1,0:T(8,128)} %get-tuple-element.31), channel_id=1, source_target_pairs={{0,4},{4,8},{8,12},{12,16},{16,20},{20,24},{24,28},{28,32},{32,36}... | collective-permute-start | bytes 1548296 | tf_op jit(solution)/shard_map/ppermute | solution.py:469
  54.0 1.9 %collective-permute-start.5 = (f32[9,14,8,128]{3,2,1,0:T(8,128)S(1)}, f32[9,14,8,128]{3,2,1,0:T(8,128)S(1)}, u32[]{:S(2)}, u32[]{:S(2)}) collective-permute-start(f32[9,14,8,128]{3,2,1,0:T(8,128)S(1)} %get-tuple-element.32), channel_id=1, source_target_pairs={{4,0},{8,4},{12,8},{16,12},{20,16},{24,20},{28,24},{32,28},{36,32}... | collective-permute-start | bytes 1548296 | tf_op jit(solution)/shard_map/ppermute | solution.py:469
  55.9 5.0 %all-to-all-done.1.m_ref = f32[4,25,16,128]{3,2,1,0:T(8,128)S(1)} async-done(((f32[4,25,16,128]{3,2,1,0:T(8,128)}), f32[4,25,16,128]{3,2,1,0:T(8,128)S(1)}, u32[]{:S(2)}, u32[]{:S(2)}) %all-to-all-start.1) | async-done | bytes 819232 | tf_op jit(solution)/shard_map/all_to_all | solution.py:506
  60.9 2.6 %evolve.1 = (f32[128,4,128]{2,1,0:T(4,128)}, f32[24,16,128]{2,1,0:T(8,128)S(1)}) custom-call(s32[4]{0:T(128)S(1)} %pad_add_fusion.pos_ref, f32[4,25,16,128]{3,2,1,0:T(8,128)S(1)} %all-to-all-done.1.m_ref, f32[25,16,128]{2,1,0:T(8,128)S(1)} %get-tuple-element.28.top_ref, f32[9,16,128]{2,1,0:T(8,128)S(1)} %get-tuple-element.34.d2_ref, ...), custom_call_target="tpu_custom_call" | custom-call | tf_op jit(solution)/shard_map/evolve/pallas_call | solution.py:447
  63.5 0.0 copy-start.8
  63.5 9.4 %all-to-all-start.2 = ((f32[128,4,128]{2,1,0:T(4,128)}), f32[128,4,128]{2,1,0:T(4,128)S(1)}, u32[]{:S(2)}, u32[]{:S(2)}) async-start(f32[128,4,128]{2,1,0:T(4,128)} %get-tuple-element.40), calls=%async_computation.2 | async-start | bytes 524288 | tf_op jit(solution)/shard_map/all_to_all | solution.py:521
  72.9 0.0 copy-start.6
  72.9 3.5 %collective-permute-start.6 = (f32[16,8,128]{2,1,0:T(8,128)S(1)}, f32[16,8,128]{2,1,0:T(8,128)S(1)}, u32[]{:S(2)}, u32[]{:S(2)}) collective-permute-start(f32[16,8,128]{2,1,0:T(8,128)S(1)} %get-tuple-element.49), channel_id=1, source_target_pairs={{0,4},{4,8},{8,12},{12,16},{16,20},{20,24},{24,28},{28,32},{32,36}... | collective-permute-start | bytes 196616 | tf_op jit(solution)/shard_map/ppermute | solution.py:469
  76.4 1.9 %collective-permute-start.7 = (f32[16,8,128]{2,1,0:T(8,128)S(1)}, f32[16,8,128]{2,1,0:T(8,128)S(1)}, u32[]{:S(2)}, u32[]{:S(2)}) collective-permute-start(f32[16,8,128]{2,1,0:T(8,128)S(1)} %get-tuple-element.48), channel_id=1, source_target_pairs={{4,0},{8,4},{12,8},{16,12},{20,16},{24,20},{28,24},{32,28},{36,32}... | collective-permute-start | bytes 196616 | tf_op jit(solution)/shard_map/ppermute | solution.py:469
  78.4 0.0 collective-permute-done.4.low2_ref
  78.4 0.0 collective-permute-done.5.high2_ref
  78.4 0.0 copy-done.8
  78.4 0.0 copy-done.6
  78.4 1.8 %pure.1 = (f32[8,4,2,8,128]{4,3,2,1,0:T(8,128)S(1)}, f32[8,6,4,8,128]{4,3,2,1,0:T(8,128)S(1)}) custom-call(s32[4]{0:T(128)S(1)} %pad_add_fusion.pos_ref, f32[9,4,2,8,128]{4,3,2,1,0:T(8,128)S(1)} %constant_dynamic-update-slice_fusion.x_ref, f32[8,4,8,128]{3,2,1,0:T(8,128)S(1)} %collective-permute-done.lo_ref, f32[8,4,8,128]{3,2,1,0:T(8,128)S(1)} %copy-done.8, ...), custom_call_target="tpu_custom_call" | custom-call | flops 10000000000 | tf_op jit(solution)/shard_map/pure/pallas_call | solution.py:447
  80.2 0.0 collective-permute-done.6.before_ref
  80.2 5.3 %collective-permute-done.7.after_ref = f32[16,8,128]{2,1,0:T(8,128)S(1)} collective-permute-done((f32[16,8,128]{2,1,0:T(8,128)S(1)}, f32[16,8,128]{2,1,0:T(8,128)S(1)}, u32[]{:S(2)}, u32[]{:S(2)}) %collective-permute-start.7) | collective-permute-done | bytes 65568 | tf_op jit(solution)/shard_map/ppermute | solution.py:469
  85.5 0.8 last.1
  86.3 0.8 reshape.26
  87.2 0.0 copy-start
  87.2 0.0 copy-start.2
  87.2 0.0 copy-start.4
  87.2 0.8 reshape.27
  88.0 6.8 %all-to-all-done.2.back_ref = f32[128,4,128]{2,1,0:T(4,128)S(1)} async-done(((f32[128,4,128]{2,1,0:T(4,128)}), f32[128,4,128]{2,1,0:T(4,128)S(1)}, u32[]{:S(2)}, u32[]{:S(2)}) %all-to-all-start.2) | async-done | bytes 262176 | tf_op jit(solution)/shard_map/all_to_all | solution.py:521
  94.8 0.0 copy-done
  94.8 0.0 copy-done.2
  94.8 0.0 copy-done.4
  94.8 2.0 %adatoms.1 = (f32[40,2,768]{2,1,0:T(2,128)}, f32[40,2,768]{2,1,0:T(2,128)}) custom-call(f32[40,2,768]{2,1,0:T(2,128)S(1)} %copy-done, f32[128,4,128]{2,1,0:T(4,128)S(1)} %all-to-all-done.2.back_ref, s32[1,768]{1,0:T(1,128)S(1)} %bitcast.12, s32[1,768]{1,0:T(1,128)S(1)} %copy-done.4, f32[40,40]{1,0:T(8,128)S(1)} %copy-done.1, f32[4,40]{1,0:T(4,128)S(1)} %copy-done.3), custom_call_target="tpu_custom_call" | custom-call | tf_op jit(solution)/shard_map/adatoms/pallas_call | solution.py:447
  (6 shorter events, 0.1 us)
Async XLA Ops:
  3.3 19.8 %copy-start.9 = (f32[4,2,4,2,1024]{4,3,2,1,0:T(2,128)S(1)}, f32[4,2,4,2,1024]{4,3,2,1,0:T(2,128)}, u32[]{:S(2)}) copy-start(f32[4,2,4,2,1024]{4,3,2,1,0:T(2,128)} %param.7) | copy-start | bytes 786436
  3.3 38.8 %all-to-all-start = ((f32[128,1,384]{2,1,0:T(1,128)}), f32[128,1,384]{2,1,0:T(1,128)S(1)}, u32[]{:S(2)}, u32[]{:S(2)}) async-start(f32[128,1,384]{2,1,0:T(1,128)} %get-tuple-element.27), calls=%async_computation | async-start | bytes 393216 | tf_op jit(solution)/shard_map/all_to_all | solution.py:483
  23.4 5.3 %copy-start.10 = (f32[4,2,1024]{2,1,0:T(2,128)S(1)}, f32[4,2,1024]{2,1,0:T(2,128)}, u32[]{:S(2)}) copy-start(f32[4,2,1024]{2,1,0:T(2,128)} %param.9) | copy-start | bytes 98308
  23.4 10.0 %collective-permute-start = (f32[8,4,8,128]{3,2,1,0:T(8,128)S(1)}, f32[8,4,8,128]{3,2,1,0:T(8,128)S(1)}, u32[]{:S(2)}, u32[]{:S(2)}) collective-permute-start(f32[8,4,8,128]{3,2,1,0:T(8,128)S(1)} %get-tuple-element.47), channel_id=1, source_target_pairs={{0,4},{4,8},{8,12},{12,16},{16,20},{20,24},{24,28},{28,32},{32,36}... | collective-permute-start | bytes 393224 | tf_op jit(solution)/shard_map/ppermute | solution.py:469
  26.8 9.4 %collective-permute-start.1 = (f32[8,4,8,128]{3,2,1,0:T(8,128)S(1)}, f32[8,4,8,128]{3,2,1,0:T(8,128)S(1)}, u32[]{:S(2)}, u32[]{:S(2)}) collective-permute-start(f32[8,4,8,128]{3,2,1,0:T(8,128)S(1)} %get-tuple-element.46), channel_id=1, source_target_pairs={{4,0},{8,4},{12,8},{16,12},{20,16},{24,20},{28,24},{32,28},{36,32}... | collective-permute-start | bytes 393224 | tf_op jit(solution)/shard_map/ppermute | solution.py:469
  28.8 7.3 %copy-start.3 = (f32[4,40]{1,0:T(4,128)S(1)}, f32[4,40]{1,0:T(4,128)}, u32[]{:S(2)}) copy-start(f32[4,40]{1,0:T(4,128)} %coup_ref.3) | copy-start | bytes 1924
  28.9 7.3 %copy-start.1 = (f32[40,40]{1,0:T(8,128)S(1)}, f32[40,40]{1,0:T(8,128)}, u32[]{:S(2)}) copy-start(f32[40,40]{1,0:T(8,128)} %block_ref.3) | copy-start | bytes 19204
  28.9 19.8 %collective-permute-start.2 = (f32[9,3,2,8,128]{4,3,2,1,0:T(8,128)S(1)}, f32[9,3,2,8,128]{4,3,2,1,0:T(8,128)S(1)}, u32[]{:S(2)}, u32[]{:S(2)}) collective-permute-start(f32[9,3,2,8,128]{4,3,2,1,0:T(8,128)S(1)} %get-tuple-element.45), channel_id=1, source_target_pairs={{0,1},{1,2},{2,3},{4,5},{5,6},{6,7},{8,9},{9,10},{10,11},{12,13},{... | collective-permute-start | bytes 663560 | tf_op jit(solution)/shard_map/ppermute | solution.py:469
  32.1 16.6 %collective-permute-start.3 = (f32[9,3,2,8,128]{4,3,2,1,0:T(8,128)S(1)}, f32[9,3,2,8,128]{4,3,2,1,0:T(8,128)S(1)}, u32[]{:S(2)}, u32[]{:S(2)}) collective-permute-start(f32[9,3,2,8,128]{4,3,2,1,0:T(8,128)S(1)} %get-tuple-element.44), channel_id=1, source_target_pairs={{1,0},{2,1},{3,2},{5,4},{6,5},{7,6},{9,8},{10,9},{11,10},{13,12},{... | collective-permute-start | bytes 663560 | tf_op jit(solution)/shard_map/ppermute | solution.py:469
  36.2 12.5 %copy-start.7 = (f32[8,4,8,128]{3,2,1,0:T(8,128)}, f32[8,4,8,128]{3,2,1,0:T(8,128)S(1)}, u32[]{:S(2)}) copy-start(f32[8,4,8,128]{3,2,1,0:T(8,128)S(1)} %collective-permute-done.1.hi_ref) | copy-start | bytes 393220
  44.5 16.4 %all-to-all-start.1 = ((f32[4,25,16,128]{3,2,1,0:T(8,128)}), f32[4,25,16,128]{3,2,1,0:T(8,128)S(1)}, u32[]{:S(2)}, u32[]{:S(2)}) async-start(f32[4,25,16,128]{3,2,1,0:T(8,128)} %get-tuple-element.33), calls=%async_computation.1 | async-start | bytes 1638400 | tf_op jit(solution)/shard_map/all_to_all | solution.py:506
  48.7 0.9 copy-start.5
  49.6 28.8 %collective-permute-start.4 = (f32[9,14,8,128]{3,2,1,0:T(8,128)}, f32[9,14,8,128]{3,2,1,0:T(8,128)S(1)}, u32[]{:S(2)}, u32[]{:S(2)}) collective-permute-start(f32[9,14,8,128]{3,2,1,0:T(8,128)} %get-tuple-element.31), channel_id=1, source_target_pairs={{0,4},{4,8},{8,12},{12,16},{16,20},{20,24},{24,28},{28,32},{32,36}... | collective-permute-start | bytes 1548296 | tf_op jit(solution)/shard_map/ppermute | solution.py:469
  54.0 24.4 %collective-permute-start.5 = (f32[9,14,8,128]{3,2,1,0:T(8,128)S(1)}, f32[9,14,8,128]{3,2,1,0:T(8,128)S(1)}, u32[]{:S(2)}, u32[]{:S(2)}) collective-permute-start(f32[9,14,8,128]{3,2,1,0:T(8,128)S(1)} %get-tuple-element.32), channel_id=1, source_target_pairs={{4,0},{8,4},{12,8},{16,12},{20,16},{24,20},{28,24},{32,28},{36,32}... | collective-permute-start | bytes 1548296 | tf_op jit(solution)/shard_map/ppermute | solution.py:469
  63.5 14.9 %copy-start.8 = (f32[8,4,8,128]{3,2,1,0:T(8,128)S(1)}, f32[8,4,8,128]{3,2,1,0:T(8,128)}, u32[]{:S(2)}) copy-start(f32[8,4,8,128]{3,2,1,0:T(8,128)} %copy-done.7) | copy-start | bytes 393220
  63.5 31.3 %all-to-all-start.2 = ((f32[128,4,128]{2,1,0:T(4,128)}), f32[128,4,128]{2,1,0:T(4,128)S(1)}, u32[]{:S(2)}, u32[]{:S(2)}) async-start(f32[128,4,128]{2,1,0:T(4,128)} %get-tuple-element.40), calls=%async_computation.2 | async-start | bytes 524288 | tf_op jit(solution)/shard_map/all_to_all | solution.py:521
  72.9 5.5 %copy-start.6 = (f32[9,3,2,8,128]{4,3,2,1,0:T(8,128)S(1)}, f32[9,3,2,8,128]{4,3,2,1,0:T(8,128)}, u32[]{:S(2)}) copy-start(f32[9,3,2,8,128]{4,3,2,1,0:T(8,128)} %copy-done.5) | copy-start | bytes 663556
  72.9 7.3 %collective-permute-start.6 = (f32[16,8,128]{2,1,0:T(8,128)S(1)}, f32[16,8,128]{2,1,0:T(8,128)S(1)}, u32[]{:S(2)}, u32[]{:S(2)}) collective-permute-start(f32[16,8,128]{2,1,0:T(8,128)S(1)} %get-tuple-element.49), channel_id=1, source_target_pairs={{0,4},{4,8},{8,12},{12,16},{16,20},{20,24},{24,28},{28,32},{32,36}... | collective-permute-start | bytes 196616 | tf_op jit(solution)/shard_map/ppermute | solution.py:469
  76.4 9.1 %collective-permute-start.7 = (f32[16,8,128]{2,1,0:T(8,128)S(1)}, f32[16,8,128]{2,1,0:T(8,128)S(1)}, u32[]{:S(2)}, u32[]{:S(2)}) collective-permute-start(f32[16,8,128]{2,1,0:T(8,128)S(1)} %get-tuple-element.48), channel_id=1, source_target_pairs={{4,0},{8,4},{12,8},{16,12},{20,16},{24,20},{28,24},{32,28},{36,32}... | collective-permute-start | bytes 196616 | tf_op jit(solution)/shard_map/ppermute | solution.py:469
  87.2 7.6 %copy-start = (f32[40,2,768]{2,1,0:T(2,128)S(1)}, f32[40,2,768]{2,1,0:T(2,128)}, u32[]{:S(2)}) copy-start(f32[40,2,768]{2,1,0:T(2,128)} %a_ref.1) | copy-start | bytes 737284
  87.2 7.6 %copy-start.2 = (s32[768,1]{0,1:T(1,128)S(1)}, s32[768,1]{0,1:T(1,128)}, u32[]{:S(2)}) copy-start(s32[768,1]{0,1:T(1,128)} %param.12) | copy-start | bytes 9220
  87.2 7.6 %copy-start.4 = (s32[1,768]{1,0:T(1,128)S(1)}, s32[1,768]{1,0:T(1,128)}, u32[]{:S(2)}) copy-start(s32[1,768]{1,0:T(1,128)} %get-tuple-element.41.rank_ref) | copy-start | bytes 9220
